TPU v7x, 32 devices: a whole 2x2x4 slice. The times are simulated.
32 devices in a mesh: lon: 8 (over z, x), lat: 4 (over y, core).
Axes of the slice: x: 2, y: 2, z: 4, core: 2. Of those that a mesh axis runs over, the one named last changes fastest.
Arguments:
- fields: float32 [6, 4, 512, 1024], P(None, None, 'lat', 'lon'), may hold values from -6 to 6
- face_weights: float32 [2, 512, 1024], P(None, 'lat', 'lon'), may hold values from 0.5 to 1.5
- inv_area: float32 [512, 1024], P('lat', 'lon'), may hold values from 0.5 to 1.5
- cell_mask: int32 [512, 1024], P('lat', 'lon'), may hold values 0 or 1
- land_blocks: int32 [4, 8], P('lat', 'lon'), may hold values 0 or 1
Outputs:
- new_fields: float32 [6, 4, 512, 1024], P(None, None, 'lat', 'lon')
All inputs are finite; a program needn't handle non-finite values. No bound on the sum of `cell_mask` or of `land_blocks` on one device may be relied on, other than what follows from the above.
Results may differ from a plain program's by a relative error of at most 0.00002.
Values sent between devices are 32-bit elements; how exact they have to be, the bound alone decides.
A program may use at most 64 MiB of HBM per device.

v0:
```python
import jax
import jax.numpy as jnp
from jax import lax
from jax.sharding import PartitionSpec as P

TIME_STEP = 0.1
ADVECTION = 0.5


def swapped(value, axis, bit):
    mask = 2**bit
    pairs = [(source, source ^ mask) for source in range(lax.axis_size(axis))]
    return lax.ppermute(value, axis, pairs)


def with_halo(cells, sides, width, closed):
    for axis, dim in sides:
        count = lax.axis_size(axis)
        ends = count if closed else count - 1
        head = lax.slice_in_dim(cells, 0, width, axis=dim)
        tail = lax.slice_in_dim(cells, cells.shape[dim] - width, cells.shape[dim], axis=dim)
        cells = jnp.concatenate(
            [
                lax.ppermute(tail, axis, [(i, (i + 1) % count) for i in range(ends)]),
                cells,
                lax.ppermute(head, axis, [((i + 1) % count, i) for i in range(ends)]),
            ],
            axis=dim,
        )
    return cells


def face_flux(near_side, far_side, face_speed, face_weight):
    return face_weight * (
        ADVECTION * face_speed * (near_side + far_side) * 0.5 - (far_side - near_side)
    )


def tendency(lon_fields, lat_fields, east_ext, north_ext, inv_area):
    u_speed = lon_fields[4]
    east_speed = 0.5 * (u_speed[..., :-1] + u_speed[..., 1:])
    flux_east = face_flux(lon_fields[..., :-1], lon_fields[..., 1:], east_speed, east_ext)
    v_speed = lat_fields[5]
    north_speed = 0.5 * (v_speed[:, :-1, :] + v_speed[:, 1:, :])
    flux_north = face_flux(
        lat_fields[:, :, :-1, :], lat_fields[:, :, 1:, :], north_speed, north_ext
    )
    return inv_area * (
        flux_east[..., :-1]
        - flux_east[..., 1:]
        + (flux_north[:, :, :-1, :] - flux_north[:, :, 1:, :])
    )


def mirror_row(top_row):
    bit_total = lax.axis_size("lon").bit_length() - 1
    bit_order = list(range(bit_total))
    partner_row = top_row
    for bit_number in bit_order:
        partner_row = swapped(partner_row, "lon", bit_number)
    return partner_row[:, ::-1]


def advance_tile(values, lon_planes, lat_planes, east_ext, north_ext, area, mask, nfield, nlevel):
    shape_out = values.shape
    lon_fields = lon_planes.reshape((nfield, nlevel) + lon_planes.shape[1:])
    lat_fields = lat_planes.reshape((nfield, nlevel) + lat_planes.shape[1:])
    change = tendency(lon_fields, lat_fields, east_ext, north_ext, area)
    return values + TIME_STEP * mask * change.reshape(shape_out)


def local(fields, face_weights, inv_area, cell_mask, land_blocks):
    nfield, nlevel, row_count, col_count = fields.shape
    plane_count = nfield * nlevel
    is_top = lax.axis_index("lat") == lax.axis_size("lat") - 1
    is_bottom = lax.axis_index("lat") == 0
    ocean_mask = cell_mask.astype(jnp.float32) * (1 - land_blocks[0, 0]).astype(jnp.float32)
    flip_sign = jnp.where(jnp.arange(plane_count) // nlevel >= 4, -1.0, 1.0).astype(jnp.float32)[
        :, None
    ]
    planes = fields.reshape(plane_count, row_count, col_count)
    sending = jnp.concatenate([planes, face_weights, inv_area[None], ocean_mask[None]], axis=0)
    widened = with_halo(sending, (("lon", 2),), 2, True)
    extended = with_halo(widened, (("lat", 1),), 2, False)
    state = extended[:plane_count]
    east_weight = extended[plane_count]
    north_weight = extended[plane_count + 1]
    area_ext = extended[plane_count + 2]
    mask_ext = extended[plane_count + 3]
    first_fold = mirror_row(state[:, row_count + 1, :])
    north_row = jnp.where(is_top, first_fold * flip_sign, state[:, row_count + 2, :])
    state = state.at[:, row_count + 2, :].set(north_row)
    margin = advance_tile(
        state[:, 1 : row_count + 3, 1 : col_count + 3],
        state[:, 1 : row_count + 3, :],
        state[:, :, 1 : col_count + 3],
        east_weight[1 : row_count + 3, 0 : col_count + 3],
        north_weight[0 : row_count + 3, 1 : col_count + 3],
        area_ext[1 : row_count + 3, 1 : col_count + 3],
        mask_ext[1 : row_count + 3, 1 : col_count + 3],
        nfield,
        nlevel,
    )
    margin = margin.at[:, 0, :].set(jnp.where(is_bottom, 0.0, margin[:, 0, :]))
    second_fold = mirror_row(margin[:, row_count, :])
    upper_row = jnp.where(is_top, second_fold * flip_sign, margin[:, row_count + 1, :])
    margin = margin.at[:, row_count + 1, :].set(upper_row)
    result = advance_tile(
        margin[:, 1 : row_count + 1, 1 : col_count + 1],
        margin[:, 1 : row_count + 1, :],
        margin[:, :, 1 : col_count + 1],
        east_weight[2 : row_count + 2, 1 : col_count + 2],
        north_weight[1 : row_count + 2, 2 : col_count + 2],
        area_ext[2 : row_count + 2, 2 : col_count + 2],
        mask_ext[2 : row_count + 2, 2 : col_count + 2],
        nfield,
        nlevel,
    )
    return result.reshape(nfield, nlevel, row_count, col_count)


def solution(mesh):
    in_specs = (
        P(None, None, "lat", "lon"),
        P(None, "lat", "lon"),
        P("lat", "lon"),
        P("lat", "lon"),
        P("lat", "lon"),
    )
    out_specs = P(None, None, "lat", "lon")
    return jax.shard_map(local, mesh=mesh, in_specs=in_specs, out_specs=out_specs, check_vma=False)
```

profile of v0, /device:TPU:12, one launch (start us, length us, event | category | flops | bytes accessed | tf_op | source)
XLA Modules:
  0.0 74.1 jit_solution(6984235874584590851)
XLA Ops:
  0.0 1.9 %copy.16 = f32[6,4,128,128]{2,3,1,0:T(8,128)S(1)} copy(f32[6,4,128,128]{3,2,1,0:T(8,128)} %param.11) | data formatting | bytes 3145728 | tf_op args[0]
  1.9 0.9 %copy.18 = s32[128,128]{0,1:T(8,128)S(1)} copy(s32[128,128]{1,0:T(8,128)} %param.14) | data formatting | bytes 131072 | tf_op args[3]
  3.5 0.1 copy.19
  3.7 0.1 copy.17
  3.8 1.5 %collective-permute-start = (f32[28,128,2]{1,2,0:T(2,128)S(1)}, f32[28,128,2]{1,2,0:T(2,128)S(1)}, u32[]{:S(2)}, u32[]{:S(2)}) collective-permute-start(f32[28,128,2]{1,2,0:T(2,128)S(1)} %get-tuple-element.47), channel_id=1, source_target_pairs={{0,4},{4,8},{8,12},{12,16},{16,20},{20,24},{24,28},{28,0},{1,5},{5... | collective-permute-start | bytes 86024 | tf_op jit(solution)/shard_map/ppermute | solution.py:24
  5.4 1.4 %collective-permute-start.1 = (f32[28,128,2]{1,2,0:T(2,128)S(1)}, f32[28,128,2]{1,2,0:T(2,128)S(1)}, u32[]{:S(2)}, u32[]{:S(2)}) collective-permute-start(f32[28,128,2]{1,2,0:T(2,128)S(1)} %get-tuple-element.48), channel_id=1, source_target_pairs={{4,0},{8,4},{12,8},{16,12},{20,16},{24,20},{28,24},{0,28},{5,1},{9... | collective-permute-start | bytes 86024 | tf_op jit(solution)/shard_map/ppermute | solution.py:26
  6.8 1.8 %collective-permute-done = f32[28,128,2]{1,2,0:T(2,128)S(1)} collective-permute-done((f32[28,128,2]{1,2,0:T(2,128)S(1)}, f32[28,128,2]{1,2,0:T(2,128)S(1)}, u32[]{:S(2)}, u32[]{:S(2)}) %collective-permute-start) | collective-permute-done | bytes 28704 | tf_op jit(solution)/shard_map/ppermute | solution.py:24
  8.6 0.6 collective-permute-done.1
  9.2 1.1 %pad_maximum_fusion.1 = f32[28,128,132]{1,2,0:T(8,128)S(1)} fusion(f32[28,128,2]{1,2,0:T(2,128)S(1)} %collective-permute-done.1, f32[1,128,128]{1,2,0:T(8,128)S(1)} %multiply_bitcast_fusion, f32[1,128,128]{1,2,0:T(8,128)} %bitcast.49, f32[2,128,128]{1,2,0:T(8,128)} %copy-done.3, f32[24,128,128]{1,2,0:T(8,128)S(1)} %bitcast.47, ...), kind=kLoop, calls=%fused_computation.10 | loop fusion | flops 2365440 | bytes 3784704 | tf_op jit(solution)/shard_map/concatenate | solution.py:22
  10.3 1.7 %slice.295 = f32[24,1,132]{1,2,0:T(8,128)} slice(f32[28,128,132]{1,2,0:T(8,128)S(1)} %pad_maximum_fusion.1), slice={[0:24], [127:128], [0:132]} | slice | bytes 25344 | tf_op jit(solution)/shard_map/slice | solution.py:90
  12.1 2.3 %copy.28 = f32[24,1,132]{2,0,1:T(8,128)S(1)} copy(f32[24,1,132]{1,2,0:T(8,128)} %slice.295) | data formatting | bytes 25344
  14.4 2.5 %collective-permute-start.4 = (f32[24,132]{1,0:T(8,128)S(1)}, f32[24,132]{1,0:T(8,128)S(1)}, u32[]{:S(2)}, u32[]{:S(2)}) collective-permute-start(f32[24,132]{1,0:T(8,128)S(1)} %bitcast.52), channel_id=1, source_target_pairs={{0,4},{4,0},{8,12},{12,8},{16,20},{20,16},{24,28},{28,24},{1,5},{5... | collective-permute-start | bytes 38024 | tf_op jit(solution)/shard_map/ppermute | solution.py:13
  16.9 2.5 %copy.20 = f32[28,128,132]{2,1,0:T(8,128)} copy(f32[28,128,132]{1,2,0:T(8,128)S(1)} %pad_maximum_fusion.1) | data formatting | bytes 3784704 | tf_op jit(solution)/shard_map/concatenate | solution.py:22
  19.4 1.0 %slice.292 = f32[28,2,132]{2,1,0:T(2,128)S(1)} slice(f32[28,128,132]{2,1,0:T(8,128)} %copy.20), slice={[0:28], [126:128], [0:132]} | slice | bytes 59136 | tf_op jit(solution)/shard_map/slice | solution.py:21
  20.3 1.9 %collective-permute-start.2 = (f32[28,2,132]{2,1,0:T(2,128)S(1)}, f32[28,2,132]{2,1,0:T(2,128)S(1)}, u32[]{:S(2)}, u32[]{:S(2)}) collective-permute-start(f32[28,2,132]{2,1,0:T(2,128)S(1)} %slice.292), channel_id=1, source_target_pairs={{0,1},{1,2},{2,3},{4,5},{5,6},{6,7},{8,9},{9,10},{10,11},{12,13},{... | collective-permute-start | bytes 88712 | tf_op jit(solution)/shard_map/ppermute | solution.py:24
  22.3 1.2 %copy.27 = f32[28,2,132]{2,0,1:T(8,128)S(1)} copy(f32[28,2,132]{1,2,0:T(8,128)S(1)} %bitcast.43) | data formatting | bytes 59136
  23.5 3.6 %collective-permute-start.3 = (f32[28,2,132]{2,0,1:T(8,128)S(1)}, f32[28,2,132]{2,0,1:T(8,128)S(1)}, u32[]{:S(2)}, u32[]{:S(2)}) collective-permute-start(f32[28,2,132]{2,0,1:T(8,128)S(1)} %copy.27), channel_id=1, source_target_pairs={{1,0},{2,1},{3,2},{5,4},{6,5},{7,6},{9,8},{10,9},{11,10},{13,12},{... | collective-permute-start | bytes 88712 | tf_op jit(solution)/shard_map/ppermute | solution.py:26
  27.1 0.5 collective-permute-start.5
  27.6 3.5 %collective-permute-done.5 = f32[24,132]{1,0:T(8,128)} collective-permute-done((f32[24,132]{1,0:T(8,128)S(1)}, f32[24,132]{1,0:T(8,128)}, u32[]{:S(2)}, u32[]{:S(2)}) %collective-permute-start.5) | collective-permute-done | bytes 12704 | tf_op jit(solution)/shard_map/ppermute | solution.py:13
  31.1 3.0 %collective-permute-start.6 = (f32[24,132]{1,0:T(8,128)}, f32[24,132]{1,0:T(8,128)}, u32[]{:S(2)}, u32[]{:S(2)}) collective-permute-start(f32[24,132]{1,0:T(8,128)} %collective-permute-done.5), channel_id=1, source_target_pairs={{0,16},{4,20},{8,24},{12,28},{16,0},{20,4},{24,8},{28,12},{1,17},{... | collective-permute-start | bytes 38024 | tf_op jit(solution)/shard_map/ppermute | solution.py:13
  34.2 1.2 %maximum_bitcast_fusion.3 = (f32[132,132]{1,0:T(8,128)S(1)}, f32[132,132]{1,0:T(8,128)S(1)}, f32[132,132]{1,0:T(8,128)S(1)}, f32[132,132]{1,0:T(8,128)S(1)}) fusion(f32[28,2,132]{2,1,0:T(2,128)S(1)} %copy.23, f32[28,128,132]{2,1,0:T(8,128)} %copy.20, f32[28,2,132]{2,1,0:T(2,128)S(1)} %collective-permute-done.2), kind=kLoop, calls=%fused_computation.30 | loop fusion | flops 139392 | bytes 2230272 | tf_op jit(solution)/shard_map/squeeze | solution.py:89
  35.4 0.6 copy-done.6
  36.0 0.8 %slice_multiply_fusion = f32[130,130]{1,0:T(8,128)} fusion(f32[132,132]{1,0:T(8,128)S(1)} %get-tuple-element.41), kind=kLoop, calls=%fused_computation.29 | loop fusion | flops 16900 | bytes 135200 | tf_op jit(solution)/shard_map/mul | solution.py:69
  36.8 0.5 pad_maximum_fusion
  37.3 0.2 slice.294
  37.5 0.7 slice.300
  38.1 0.8 %slice.308 = f32[131,130]{1,0:T(8,128)} slice(f32[132,132]{1,0:T(8,128)S(1)} %get-tuple-element.42), slice={[0:131], [1:131]} | slice | bytes 136240 | tf_op jit(solution)/shard_map/slice | solution.py:98
  38.9 0.7 %slice.299 = f32[130,130]{1,0:T(8,128)} slice(f32[132,132]{1,0:T(8,128)S(1)} %get-tuple-element.44), slice={[1:131], [1:131]} | slice | bytes 135200 | tf_op jit(solution)/shard_map/slice | solution.py:99
  39.7 1.4 %reverse = f32[24,256]{1,0:T(8,128)} reverse(f32[24,256]{1,0:T(8,128)} %bitcast.37), dimensions={1} | reverse | bytes 49152
  41.1 0.8 %fusion.8 = f32[24,132]{1,0:T(8,128)S(1)} fusion(f32[28,2,132]{2,0,1:T(8,128)S(1)} %collective-permute-done.3, f32[24]{0:T(128)S(1)} %compare_select_fusion, pred[]{:T(512)S(6)} %eq.6, f32[24,256]{1,0:T(8,128)} %reverse), kind=kLoop, calls=%fused_computation.39 | loop fusion | flops 6336 | bytes 38113 | tf_op jit(solution)/shard_map/jit(_where)/select_n | solution.py:91
  42.0 0.3 scatter.10
  42.3 0.2 slice.303
  42.5 0.2 fusion.5
  42.7 0.9 %slice.311 = f32[24,132,130]{2,1,0:T(8,128)S(1)} slice(f32[24,132,132]{2,1,0:T(8,128)S(1)} %scatter.10), slice={[0:24], [0:132], [1:131]} | slice | bytes 3294720 | tf_op jit(solution)/shard_map/slice | solution.py:96
  43.7 0.4 fusion.4
  44.1 0.9 %subtract_multiply_fusion.1 = f32[6,4,130,131]{3,2,1,0:T(8,128)S(1)} fusion(f32[6,4,130,132]{3,2,1,0:T(8,128)S(1)} %bitcast.42, f32[4,130,131]{2,1,0:T(8,128)S(1)} %fusion.5, f32[130,131]{1,0:T(8,128)S(1)} %copy-done.10), kind=kLoop, calls=%fused_computation.8 | loop fusion | flops 2452320 | bytes 5245240 | tf_op jit(solution)/shard_map/mul | solution.py:34
  45.0 0.9 %subtract_multiply_fusion = f32[6,4,131,130]{3,2,1,0:T(8,128)S(1)} fusion(f32[6,4,132,130]{3,2,1,0:T(8,128)S(1)} %bitcast.41, f32[4,131,130]{2,1,0:T(8,128)S(1)} %fusion.4, f32[131,130]{1,0:T(8,128)S(1)} %copy-done.9), kind=kLoop, calls=%fused_computation.7 | loop fusion | flops 2452320 | bytes 5245240 | tf_op jit(solution)/shard_map/mul | solution.py:34
  45.9 0.0 copy-done.11
  45.9 0.9 %fusion.1 = f32[6,4,130,130]{3,2,1,0:T(8,128)S(1)} fusion(f32[6,4,131,130]{3,2,1,0:T(8,128)S(1)} %subtract_multiply_fusion, f32[6,4,130,131]{3,2,1,0:T(8,128)S(1)} %subtract_multiply_fusion.1, f32[130,130]{1,0:T(8,128)S(1)} %copy-done.11), kind=kLoop, calls=%fused_computation.3 | loop fusion | flops 1622400 | bytes 8179600 | tf_op jit(solution)/shard_map/mul | solution.py:48
  46.9 1.0 %slice_add_fusion = f32[24,130,130]{2,1,0:T(8,128)S(1)} fusion(f32[24,132,132]{2,1,0:T(8,128)S(1)} %scatter.10, f32[6,4,130,130]{3,2,1,0:T(8,128)S(1)} %fusion.1, f32[130,130]{1,0:T(8,128)S(1)} %copy-done.8), kind=kLoop, calls=%fused_computation.5 | loop fusion | flops 811200 | bytes 4934800 | tf_op jit(solution)/shard_map/add | solution.py:69
  47.9 1.7 %copy-done = f32[24,130,130]{2,1,0:T(8,128)} copy-done((f32[24,130,130]{2,1,0:T(8,128)}, f32[24,130,130]{2,1,0:T(8,128)S(1)}, u32[]{:S(2)}) %copy-start) | copy-done | bytes 1622424
  49.6 1.7 %scatter.11 = f32[24,130,130]{2,1,0:T(8,128)} dynamic-update-slice(f32[24,130,130]{2,1,0:T(8,128)} %copy-done, f32[24,1,130]{2,1,0:T(1,128)S(1)} %broadcast_select_fusion, s32[]{:T(128)} %constant.122.clone.1, s32[]{:T(128)} %constant.122.clone.1, s32[]{:T(128)} %constant.122.clone.1) | dynamic-update-slice | bytes 24964 | tf_op jit(solution)/shard_map/scatter | solution.py:104
  51.3 1.1 %fusion.10 = (f32[24,1,130]{2,1,0:T(1,128)S(1)}, f32[24,1,130]{2,1,0:T(1,128)S(1)}) fusion(f32[24,130,130]{2,1,0:T(8,128)} %scatter.11), kind=kLoop, calls=%fused_computation.48 | loop fusion | bytes 49920 | tf_op jit(solution)/shard_map/slice | solution.py:105
  52.3 0.1 collective-permute-start.7
  52.4 3.8 %collective-permute-done.7 = f32[24,130]{1,0:T(8,128)S(1)} collective-permute-done((f32[24,130]{1,0:T(8,128)S(1)}, f32[24,130]{1,0:T(8,128)S(1)}, u32[]{:S(2)}, u32[]{:S(2)}) %collective-permute-start.7) | collective-permute-done | bytes 12512 | tf_op jit(solution)/shard_map/ppermute | solution.py:13
  56.2 0.0 collective-permute-start.8
  56.2 3.8 %collective-permute-done.8 = f32[24,130]{1,0:T(8,128)S(1)} collective-permute-done((f32[24,130]{1,0:T(8,128)S(1)}, f32[24,130]{1,0:T(8,128)S(1)}, u32[]{:S(2)}, u32[]{:S(2)}) %collective-permute-start.8) | collective-permute-done | bytes 12512 | tf_op jit(solution)/shard_map/ppermute | solution.py:13
  60.1 1.0 %slice_multiply_fusion.1 = f32[128,128]{1,0:T(8,128)S(1)} fusion(f32[132,132]{1,0:T(8,128)} %copy-done.6), kind=kLoop, calls=%fused_computation.31 | loop fusion | flops 16384 | bytes 131072 | tf_op jit(solution)/shard_map/mul | solution.py:69
  61.1 0.1 slice.322
  61.2 1.0 %slice.330 = f32[129,128]{1,0:T(8,128)S(1)} slice(f32[132,132]{1,0:T(8,128)} %copy-done.4), slice={[1:130], [2:130]} | slice | bytes 132096 | tf_op jit(solution)/shard_map/slice | solution.py:113
  62.2 1.0 %slice.321 = f32[128,128]{1,0:T(8,128)S(1)} slice(f32[132,132]{1,0:T(8,128)} %copy-done.5), slice={[2:130], [2:130]} | slice | bytes 131072 | tf_op jit(solution)/shard_map/slice | solution.py:114
  63.2 1.6 %collective-permute-done.9 = f32[24,130]{1,0:T(8,128)S(1)} collective-permute-done((f32[24,130]{1,0:T(8,128)S(1)}, f32[24,130]{1,0:T(8,128)S(1)}, u32[]{:S(2)}, u32[]{:S(2)}) %collective-permute-start.9) | collective-permute-done | bytes 12512 | tf_op jit(solution)/shard_map/ppermute | solution.py:13
  64.8 0.1 reverse.1
  64.9 0.1 fusion.9
  65.0 1.7 %scatter.14 = f32[24,130,130]{2,1,0:T(8,128)} dynamic-update-slice(f32[24,130,130]{2,1,0:T(8,128)} %scatter.11, f32[24,1,130]{2,1,0:T(1,128)S(1)} %reshape.156, s32[]{:T(128)} %constant.122.clone.1, s32[]{:T(128)} %constant.133.clone.1, s32[]{:T(128)} %constant.122.clone.1) | dynamic-update-slice | bytes 24964 | tf_op jit(solution)/shard_map/scatter | solution.py:107
  66.8 2.4 %slice.325 = f32[24,128,130]{2,1,0:T(8,128)S(1)} slice(f32[24,130,130]{2,1,0:T(8,128)} %scatter.14), slice={[0:24], [1:129], [0:130]} | slice | bytes 3194880 | tf_op jit(solution)/shard_map/slice | solution.py:110
  69.2 0.5 copy-done.1
  69.7 0.2 fusion.6
  69.9 0.5 slice.333
  70.4 0.2 fusion.7
  70.6 0.9 %subtract_multiply_fusion.2 = f32[6,4,128,129]{3,2,1,0:T(8,128)S(1)} fusion(f32[6,4,128,130]{3,2,1,0:T(8,128)S(1)} %bitcast.44, f32[4,128,129]{2,1,0:T(8,128)S(1)} %fusion.6, f32[128,129]{1,0:T(8,128)S(1)} %slice.322), kind=kLoop, calls=%fused_computation.9 | loop fusion | flops 2377728 | bytes 5085696 | tf_op jit(solution)/shard_map/mul | solution.py:34
  71.5 0.4 subtract_multiply_fusion.3
  72.0 0.5 fusion.3
  72.5 1.6 %slice_add_fusion.1 = f32[24,128,128]{2,1,0:T(8,128)} fusion(f32[24,130,130]{2,1,0:T(8,128)S(1)} %copy-done.1, f32[6,4,128,128]{3,2,1,0:T(8,128)S(1)} %fusion.3, f32[128,128]{1,0:T(8,128)S(1)} %slice_multiply_fusion.1), kind=kLoop, calls=%fused_computation.16 | loop fusion | flops 786432 | bytes 4784128 | tf_op jit(solution)/shard_map/add | solution.py:69
  (37 shorter events, 0.2 us)
Async XLA Ops:
  0.0 3.5 %copy-start.12 = (f32[2,128,128]{2,1,0:T(8,128)S(1)}, f32[2,128,128]{2,1,0:T(8,128)}, u32[]{:S(2)}) copy-start(f32[2,128,128]{2,1,0:T(8,128)} %param.12) | copy-start | bytes 393220
  0.0 3.6 %copy-start.13 = (f32[128,128]{1,0:T(8,128)S(1)}, f32[128,128]{1,0:T(8,128)}, u32[]{:S(2)}) copy-start(f32[128,128]{1,0:T(8,128)} %param.13) | copy-start | bytes 196612
  3.6 5.0 %copy-start.3 = (f32[2,128,128]{1,2,0:T(8,128)}, f32[2,128,128]{1,2,0:T(8,128)S(1)}, u32[]{:S(2)}) copy-start(f32[2,128,128]{1,2,0:T(8,128)S(1)} %copy.19) | copy-start | bytes 393220
  3.8 4.9 %copy-start.7 = (f32[128,128]{0,1:T(8,128)}, f32[128,128]{0,1:T(8,128)S(1)}, u32[]{:S(2)}) copy-start(f32[128,128]{0,1:T(8,128)S(1)} %copy.17) | copy-start | bytes 196612
  3.8 4.8 %collective-permute-start = (f32[28,128,2]{1,2,0:T(2,128)S(1)}, f32[28,128,2]{1,2,0:T(2,128)S(1)}, u32[]{:S(2)}, u32[]{:S(2)}) collective-permute-start(f32[28,128,2]{1,2,0:T(2,128)S(1)} %get-tuple-element.47), channel_id=1, source_target_pairs={{0,4},{4,8},{8,12},{12,16},{16,20},{20,24},{24,28},{28,0},{1,5},{5... | collective-permute-start | bytes 86024 | tf_op jit(solution)/shard_map/ppermute | solution.py:24
  5.4 3.9 %collective-permute-start.1 = (f32[28,128,2]{1,2,0:T(2,128)S(1)}, f32[28,128,2]{1,2,0:T(2,128)S(1)}, u32[]{:S(2)}, u32[]{:S(2)}) collective-permute-start(f32[28,128,2]{1,2,0:T(2,128)S(1)} %get-tuple-element.48), channel_id=1, source_target_pairs={{4,0},{8,4},{12,8},{16,12},{20,16},{24,20},{28,24},{0,28},{5,1},{9... | collective-permute-start | bytes 86024 | tf_op jit(solution)/shard_map/ppermute | solution.py:26
  14.4 12.7 %collective-permute-start.4 = (f32[24,132]{1,0:T(8,128)S(1)}, f32[24,132]{1,0:T(8,128)S(1)}, u32[]{:S(2)}, u32[]{:S(2)}) collective-permute-start(f32[24,132]{1,0:T(8,128)S(1)} %bitcast.52), channel_id=1, source_target_pairs={{0,4},{4,0},{8,12},{12,8},{16,20},{20,16},{24,28},{28,24},{1,5},{5... | collective-permute-start | bytes 38024 | tf_op jit(solution)/shard_map/ppermute | solution.py:13
  20.3 13.9 %collective-permute-start.2 = (f32[28,2,132]{2,1,0:T(2,128)S(1)}, f32[28,2,132]{2,1,0:T(2,128)S(1)}, u32[]{:S(2)}, u32[]{:S(2)}) collective-permute-start(f32[28,2,132]{2,1,0:T(2,128)S(1)} %slice.292), channel_id=1, source_target_pairs={{0,1},{1,2},{2,3},{4,5},{5,6},{6,7},{8,9},{9,10},{10,11},{12,13},{... | collective-permute-start | bytes 88712 | tf_op jit(solution)/shard_map/ppermute | solution.py:24
  23.5 10.7 %collective-permute-start.3 = (f32[28,2,132]{2,0,1:T(8,128)S(1)}, f32[28,2,132]{2,0,1:T(8,128)S(1)}, u32[]{:S(2)}, u32[]{:S(2)}) collective-permute-start(f32[28,2,132]{2,0,1:T(8,128)S(1)} %copy.27), channel_id=1, source_target_pairs={{1,0},{2,1},{3,2},{5,4},{6,5},{7,6},{9,8},{10,9},{11,10},{13,12},{... | collective-permute-start | bytes 88712 | tf_op jit(solution)/shard_map/ppermute | solution.py:26
  27.1 4.0 %collective-permute-start.5 = (f32[24,132]{1,0:T(8,128)S(1)}, f32[24,132]{1,0:T(8,128)}, u32[]{:S(2)}, u32[]{:S(2)}) collective-permute-start(f32[24,132]{1,0:T(8,128)S(1)} %collective-permute-done.4), channel_id=1, source_target_pairs={{0,8},{4,12},{8,0},{12,4},{16,24},{20,28},{24,16},{28,20},{1,9},{5... | collective-permute-start | bytes 38024 | tf_op jit(solution)/shard_map/ppermute | solution.py:13
  27.6 9.1 %copy-start.2 = (f32[28,128,132]{2,1,0:T(8,128)S(1)}, f32[28,128,132]{2,1,0:T(8,128)}, u32[]{:S(2)}) copy-start(f32[28,128,132]{2,1,0:T(8,128)} %copy.20) | copy-start | bytes 5677060
  31.1 8.5 %collective-permute-start.6 = (f32[24,132]{1,0:T(8,128)}, f32[24,132]{1,0:T(8,128)}, u32[]{:S(2)}, u32[]{:S(2)}) collective-permute-start(f32[24,132]{1,0:T(8,128)} %collective-permute-done.5), channel_id=1, source_target_pairs={{0,16},{4,20},{8,24},{12,28},{16,0},{20,4},{24,8},{28,12},{1,17},{... | collective-permute-start | bytes 38024 | tf_op jit(solution)/shard_map/ppermute | solution.py:13
  35.4 0.7 copy-start.6
  35.4 2.8 %copy-start.4 = (f32[132,132]{1,0:T(8,128)}, f32[132,132]{1,0:T(8,128)S(1)}, u32[]{:S(2)}) copy-start(f32[132,132]{1,0:T(8,128)S(1)} %get-tuple-element.42) | copy-start | bytes 209092
  35.4 3.5 %copy-start.5 = (f32[132,132]{1,0:T(8,128)}, f32[132,132]{1,0:T(8,128)S(1)}, u32[]{:S(2)}) copy-start(f32[132,132]{1,0:T(8,128)S(1)} %get-tuple-element.44) | copy-start | bytes 209092
  42.7 1.3 %copy-start.10 = (f32[130,131]{1,0:T(8,128)S(1)}, f32[130,131]{1,0:T(8,128)}, u32[]{:S(2)}) copy-start(f32[130,131]{1,0:T(8,128)} %slice.300) | copy-start | bytes 204364
  44.0 1.0 %copy-start.9 = (f32[131,130]{1,0:T(8,128)S(1)}, f32[131,130]{1,0:T(8,128)}, u32[]{:S(2)}) copy-start(f32[131,130]{1,0:T(8,128)} %slice.308) | copy-start | bytes 204364
  45.0 0.9 %copy-start.11 = (f32[130,130]{1,0:T(8,128)S(1)}, f32[130,130]{1,0:T(8,128)}, u32[]{:S(2)}) copy-start(f32[130,130]{1,0:T(8,128)} %slice.299) | copy-start | bytes 202804
  45.9 0.9 %copy-start.8 = (f32[130,130]{1,0:T(8,128)S(1)}, f32[130,130]{1,0:T(8,128)}, u32[]{:S(2)}) copy-start(f32[130,130]{1,0:T(8,128)} %slice_multiply_fusion) | copy-start | bytes 202804
  47.9 1.7 %copy-start = (f32[24,130,130]{2,1,0:T(8,128)}, f32[24,130,130]{2,1,0:T(8,128)S(1)}, u32[]{:S(2)}) copy-start(f32[24,130,130]{2,1,0:T(8,128)S(1)} %slice_add_fusion) | copy-start | bytes 4867204
  52.3 3.9 %collective-permute-start.7 = (f32[24,130]{1,0:T(8,128)S(1)}, f32[24,130]{1,0:T(8,128)S(1)}, u32[]{:S(2)}, u32[]{:S(2)}) collective-permute-start(f32[24,130]{1,0:T(8,128)S(1)} %bitcast.51), channel_id=1, source_target_pairs={{0,4},{4,0},{8,12},{12,8},{16,20},{20,16},{24,28},{28,24},{1,5},{5... | collective-permute-start | bytes 37448 | tf_op jit(solution)/shard_map/ppermute | solution.py:13
  56.2 3.8 %collective-permute-start.8 = (f32[24,130]{1,0:T(8,128)S(1)}, f32[24,130]{1,0:T(8,128)S(1)}, u32[]{:S(2)}, u32[]{:S(2)}) collective-permute-start(f32[24,130]{1,0:T(8,128)S(1)} %collective-permute-done.7), channel_id=1, source_target_pairs={{0,8},{4,12},{8,0},{12,4},{16,24},{20,28},{24,16},{28,20},{1,9},{5... | collective-permute-start | bytes 37448 | tf_op jit(solution)/shard_map/ppermute | solution.py:13
  60.1 4.7 %collective-permute-start.9 = (f32[24,130]{1,0:T(8,128)S(1)}, f32[24,130]{1,0:T(8,128)S(1)}, u32[]{:S(2)}, u32[]{:S(2)}) collective-permute-start(f32[24,130]{1,0:T(8,128)S(1)} %collective-permute-done.8), channel_id=1, source_target_pairs={{0,16},{4,20},{8,24},{12,28},{16,0},{20,4},{24,8},{28,12},{1,17},{... | collective-permute-start | bytes 37448 | tf_op jit(solution)/shard_map/ppermute | solution.py:13
  66.8 3.0 %copy-start.1 = (f32[24,130,130]{2,1,0:T(8,128)S(1)}, f32[24,130,130]{2,1,0:T(8,128)}, u32[]{:S(2)}) copy-start(f32[24,130,130]{2,1,0:T(8,128)} %scatter.14) | copy-start | bytes 4867204
where the time goes:
time: 74.7 us; the launch traced here: 74.1 us
  local copies, waits for them, and re-layouts  29.6 us (40%)
  waiting for transfers between devices  15.2 us (20%)
  starting transfers between devices  14.7 us (20%)
  other arithmetic  13.6 us (18%)
  between operations  1.05 us (1%)
    ppermute x6, waiting for transfers between devices, swapped(): return lax.ppermute(value, axis, pairs)  12.7 us
    unnamed x37, local copies, waits for them, and re-layouts  11 us
    ppermute x6, starting transfers between devices, swapped(): return lax.ppermute(value, axis, pairs)  6.13 us
    ppermute x2, starting transfers between devices, with_halo(): lax.ppermute(head, axis, [((i + 1) % count, i) for i in range(ends)])  5.08 us
    ppermute x2, starting transfers between devices, with_halo(): lax.ppermute(tail, axis, [(i, (i + 1) % count) for i in range(ends)])  3.46 us
    mul x4, other arithmetic, face_flux(): face_weight * (ADVECTION * face_speed * (near_side + far_side) * 0.5 - (f...  3.13 us
    add x2, other arithmetic, advance_tile(): return values + TIME_STEP * mask * change.reshape(shape_out)  2.62 us
    concatenate x1, local copies, waits for them, and re-layouts, with_halo(): jnp.concatenate([lax.ppermute(tail, axis, [(i, (i + 1) % count) for i in...  2.48 us
  transfers between devices with their start and end apart: 10, of which 6 were waited for; matrix products, arithmetic and copies ran while one was open for 17% of the time, Pallas kernels for 0%

commit v1 on v0

v1 whole, which is shorter than its diff:
```python
import jax
import jax.numpy as jnp
from jax import lax
from jax.experimental import pallas as pl
from jax.experimental.pallas import tpu as pltpu
from jax.sharding import PartitionSpec as P

TIME_STEP = 0.1
PAD = 8
CHUNK = 32
LANES = 128
WEST, EAST, SOUTH, NORTH, SOUTHWEST, SOUTHEAST, NORTHWEST, NORTHEAST = range(8)


def lanes_of(shape):
    return lax.broadcasted_iota(jnp.int32, shape, len(shape) - 1)


def rows_of(shape):
    return lax.broadcasted_iota(jnp.int32, shape, len(shape) - 2)


def roll(value, shift, axis):
    return pltpu.roll(value, shift % value.shape[axis], axis)


def take_lanes(value, index):
    return jnp.take_along_axis(value, index, axis=1)


def stencil(c, x, left, right, south, north):
    c0, ce, cw, cn, cs = c
    return c0 * x + ce * right + cw * left + cn * north + cs * south


def coefficients(base, ke, kw, kn, ks, u, u_left, u_right, v, v_south, v_north):
    pe = ke * (0.125 * (u + u_right))
    pw = kw * (0.125 * (u + u_left))
    pn = kn * (0.125 * (v + v_north))
    ps = ks * (0.125 * (v + v_south))
    return base + ((pw - pe) + (ps - pn)), ke - pe, kw + pw, kn - pn, ks + ps


def kernel(
    nlon, nlat, nfield, nlevel,
    fields, face_weights, inv_area, cell_mask, land,
    out,
    ext0, ext1, obuf, weights, area, cells, scale, packed, send_s, send_n,
    recv_we, recv_ns, recv_c, halo0, halo1, coef, strips, nrows, srows, edge_rows,
    in_sems, out_sems, send_sems, recv_sems,
):
    nplane = nfield * nlevel
    rows = ext0.shape[1] - 2 * PAD
    top_row, low_row = PAD + rows, PAD - 1
    lon, lat = lax.axis_index("lon"), lax.axis_index("lat")
    is_top = lat == nlat - 1
    is_bottom = lat == 0
    east, west = lax.rem(lon + 1, nlon), lax.rem(lon + nlon - 1, nlon)
    north_lat = jnp.where(is_top, lat, lat + 1)
    north_lon = jnp.where(is_top, nlon - 1 - lon, lon)
    ne_lon = jnp.where(is_top, lax.rem(2 * nlon - 2 - lon, nlon), east)
    nw_lon = jnp.where(is_top, lax.rem(nlon - lon, nlon), west)
    ne_self = jnp.logical_and(is_top, ne_lon == lon)
    nw_self = jnp.logical_and(is_top, nw_lon == lon)
    ne_other = jnp.logical_not(ne_self)
    nw_other = jnp.logical_not(nw_self)
    not_bottom = jnp.logical_not(is_bottom)

    barrier = pltpu.get_barrier_semaphore()

    def greet(to_lon, to_lat):
        pl.semaphore_signal(
            barrier, inc=1, device_id={"lon": to_lon, "lat": to_lat},
            device_id_type=pl.DeviceIdType.MESH,
        )

    greet(west, lat)
    greet(east, lat)
    greet(north_lon, north_lat)

    @pl.when(ne_other)
    def _():
        greet(ne_lon, north_lat)

    @pl.when(nw_other)
    def _():
        greet(nw_lon, north_lat)

    @pl.when(not_bottom)
    def _():
        greet(lon, lat - 1)
        greet(east, lat - 1)
        greet(west, lat - 1)

    loads = [
        pltpu.make_async_copy(fields, ext0.at[:, pl.ds(PAD, rows), :], in_sems.at[0]),
        pltpu.make_async_copy(face_weights, weights, in_sems.at[1]),
        pltpu.make_async_copy(inv_area, area, in_sems.at[2]),
        pltpu.make_async_copy(cell_mask, cells, in_sems.at[3]),
    ]
    for load in loads:
        load.start()
    for load in loads[1:]:
        load.wait()
    sea = (1 - land[0, 0]).astype(jnp.float32)
    scale[...] = (TIME_STEP * sea) * cells[...].astype(jnp.float32) * area[...]
    loads[0].wait()

    group = lanes_of((CHUNK, LANES)) // 4
    for start in range(0, rows, CHUNK):
        piece = pl.ds(start, CHUNK)
        gathered = jnp.zeros((CHUNK, LANES), jnp.float32)
        for p in range(nplane + 3):
            if p < nplane:
                plane = ext0[p, pl.ds(PAD + start, CHUNK), :]
            elif p < nplane + 2:
                plane = weights[p - nplane, piece, :]
            else:
                plane = scale[piece, :]
            gathered = jnp.where(group == p, roll(plane, 4 * p + 2, 1), gathered)
        packed[piece, :] = gathered
    for buf, first, second, corner in ((send_s, 0, 1, 0), (send_n, rows - 1, rows - 2, rows - 8)):
        for at, row in ((0, first), (32, second)):
            for p in range(nplane):
                buf[pl.ds(at + p, 1), :] = ext0[p, pl.ds(PAD + row, 1), :]
            for i in range(2):
                buf[pl.ds(at + nplane + i, 1), :] = weights[i, pl.ds(row, 1), :]
            buf[pl.ds(at + nplane + 2, 1), :] = scale[pl.ds(row, 1), :]
            buf[pl.ds(at + nplane + 3, 5), :] = jnp.zeros((5, LANES), jnp.float32)
        buf[pl.ds(64, 8), :] = packed[pl.ds(corner, 8), :]

    def remote(src, dst, number, slot, to_lon, to_lat):
        return pltpu.make_async_remote_copy(
            src_ref=src, dst_ref=dst, send_sem=send_sems.at[number], recv_sem=recv_sems.at[slot],
            device_id={"lon": to_lon, "lat": to_lat}, device_id_type=pl.DeviceIdType.MESH,
        )

    corner_s, corner_n = send_s.at[pl.ds(64, 8), :], send_n.at[pl.ds(64, 8), :]
    go_w = remote(packed, recv_we.at[1], 0, EAST, west, lat)
    go_e = remote(packed, recv_we.at[0], 1, WEST, east, lat)
    go_n = remote(
        send_n, recv_ns.at[jnp.where(is_top, 1, 0)], 2,
        jnp.where(is_top, NORTH, SOUTH), north_lon, north_lat,
    )
    go_ne = remote(
        corner_n, recv_c.at[jnp.where(is_top, 3, 0)], 3,
        jnp.where(is_top, NORTHEAST, SOUTHWEST), ne_lon, north_lat,
    )
    go_nw = remote(
        corner_n, recv_c.at[jnp.where(is_top, 2, 1)], 4,
        jnp.where(is_top, NORTHWEST, SOUTHEAST), nw_lon, north_lat,
    )
    go_s = remote(send_s, recv_ns.at[1], 5, NORTH, lon, lat - 1)
    go_se = remote(corner_s, recv_c.at[2], 6, NORTHWEST, east, lat - 1)
    go_sw = remote(corner_s, recv_c.at[3], 7, NORTHEAST, west, lat - 1)

    greetings = 3 + jnp.where(ne_self, 0, 1) + jnp.where(nw_self, 0, 1) + jnp.where(is_bottom, 0, 3)
    pl.semaphore_wait(barrier, greetings)
    go_w.start()
    go_e.start()
    go_n.start()

    @pl.when(ne_other)
    def _():
        go_ne.start()

    @pl.when(nw_other)
    def _():
        go_nw.start()

    @pl.when(not_bottom)
    def _():
        go_s.start()
        go_se.start()
        go_sw.start()

    @pl.when(ne_self)
    def _():
        recv_c[3] = send_n[pl.ds(64, 8), :]

    @pl.when(nw_self)
    def _():
        recv_c[2] = send_n[pl.ds(64, 8), :]

    @pl.when(is_bottom)
    def _():
        recv_ns[0] = jnp.zeros(recv_ns.shape[1:], jnp.float32)
        recv_c[0] = jnp.zeros(recv_c.shape[1:], jnp.float32)
        recv_c[1] = jnp.zeros(recv_c.shape[1:], jnp.float32)

    def arrived(dst, slot):
        remote(dst, dst, 0, slot, west, lat).wait_recv()

    arrived(recv_we.at[0], WEST)
    arrived(recv_we.at[1], EAST)
    arrived(recv_ns.at[1], NORTH)

    @pl.when(not_bottom)
    def _():
        arrived(recv_ns.at[0], SOUTH)
        arrived(recv_c.at[0], SOUTHWEST)
        arrived(recv_c.at[1], SOUTHEAST)

    @pl.when(ne_other)
    def _():
        arrived(recv_c.at[3], NORTHEAST)

    @pl.when(nw_other)
    def _():
        arrived(recv_c.at[2], NORTHWEST)

    go_w.wait_send()
    go_e.wait_send()
    go_n.wait_send()

    @pl.when(ne_other)
    def _():
        go_ne.wait_send()

    @pl.when(nw_other)
    def _():
        go_nw.wait_send()

    @pl.when(not_bottom)
    def _():
        go_s.wait_send()
        go_se.wait_send()
        go_sw.wait_send()

    def at_top(shape):
        return jnp.full(shape, lat, jnp.int32) == nlat - 1

    shape = (64, LANES)
    came = recv_ns[1, pl.ds(0, 64), :]
    sub = rows_of(shape) % 32
    flips = jnp.where(jnp.logical_and(sub >= 4 * nlevel, sub < nplane), -1.0, 1.0)
    nrows[...] = jnp.where(
        at_top(shape), flips * take_lanes(came, LANES - 1 - lanes_of(shape)), came
    )
    srows[...] = recv_ns[0, pl.ds(0, 64), :]
    for p in range(nplane):
        ext0[p, pl.ds(top_row, 1), :] = nrows[pl.ds(p, 1), :]
        ext0[p, pl.ds(low_row, 1), :] = srows[pl.ds(p, 1), :]

    eight = (8, LANES)
    lane8 = lanes_of(eight)
    slot8 = lane8 % 4
    flip8 = jnp.where(jnp.logical_and(lane8 >= 16 * nlevel, lane8 < 4 * nplane), -1.0, 1.0)
    east8 = lane8 // 4 == nplane

    def beyond(block):
        upside = jnp.concatenate([block[7 - i : 8 - i, :] for i in range(8)], axis=0)
        mirrored = flip8 * take_lanes(upside, lane8 - slot8 + (3 - slot8))
        mirrored = jnp.where(east8, roll(mirrored, -1, 1), mirrored)
        return mirrored

    middle_n = recv_ns[1, pl.ds(64, 8), :]
    middle_s = recv_ns[0, pl.ds(64, 8), :]
    slot = lanes_of((rows, LANES)) % 4
    strips[0, pl.ds(PAD, rows), :] = jnp.where(slot < 2, recv_we[0], packed[...])
    strips[1, pl.ds(PAD, rows), :] = jnp.where(slot < 2, packed[...], recv_we[1])
    strips[0, pl.ds(0, 8), :] = jnp.where(slot8 < 2, recv_c[0], middle_s)
    strips[1, pl.ds(0, 8), :] = jnp.where(slot8 < 2, middle_s, recv_c[1])
    for side in range(2):
        lower, upper = ((recv_c[2], middle_n), (middle_n, recv_c[3]))[side]
        strips[side, pl.ds(top_row, 8), :] = jnp.where(
            at_top(eight),
            beyond(jnp.where(slot8 >= 2, lower, upper)),
            jnp.where(slot8 < 2, lower, upper),
        )

    tall = (rows + 2 * PAD, LANES)
    slot_t = lanes_of(tall) % 4
    lane_t = lanes_of(tall)
    folded = jnp.logical_and(at_top(tall), rows_of(tall) == top_row)

    def halo_of(west_strip, east_strip):
        return jnp.where(slot_t == 1, west_strip, roll(east_strip, -2, 1))

    advanced = []
    for side in range(2):
        x = strips[side]
        u = take_lanes(x, 16 * nlevel + lane_t % (4 * nlevel))
        v = take_lanes(x, 20 * nlevel + lane_t % (4 * nlevel))
        e_weight, n_weight, k = (
            take_lanes(x, 4 * (nplane + i) + slot_t) for i in range(3)
        )
        n_behind = roll(n_weight, 1, 0)
        n_south = jnp.where(folded, n_weight, n_behind)
        n_north = jnp.where(folded, roll(n_weight, -1, 0), n_weight)
        ke, kw, kn, ks = k * e_weight, k * roll(e_weight, 1, 1), k * n_north, k * n_south
        base = 1.0 - ((ke + kw) + (kn + ks))
        c = coefficients(
            base, ke, kw, kn, ks,
            u, roll(u, 1, 1), roll(u, -1, 1), v, roll(v, 1, 0), roll(v, -1, 0),
        )
        advanced.append(
            stencil(c, x, roll(x, 1, 1), roll(x, -1, 1), roll(x, 1, 0), roll(x, -1, 0))
        )
    halo0[...] = halo_of(strips[0], strips[1])
    halo1[...] = halo_of(advanced[0], advanced[1])

    lane_c = lanes_of((CHUNK, LANES))
    for start in range(0, rows, CHUNK):
        piece = pl.ds(start, CHUNK)
        k = scale[piece, :]
        e_weight = weights[0, piece, :]
        n_weight = weights[1, piece, :]
        outer = roll(strips[0, pl.ds(PAD + start, CHUNK), :], -(4 * nplane + 1), 1)
        w_weight = jnp.where(lane_c == 0, outer, roll(e_weight, 1, 1))
        if start:
            s_weight = weights[1, pl.ds(start - 1, CHUNK), :]
        else:
            s_weight = jnp.where(
                rows_of((CHUNK, LANES)) == 0, srows[pl.ds(nplane + 1, 1), :], roll(n_weight, 1, 0)
            )
        ke, kw, kn, ks = k * e_weight, k * w_weight, k * n_weight, k * s_weight
        coef[0, piece, :] = 1.0 - ((ke + kw) + (kn + ks))
        coef[1, piece, :] = ke
        coef[2, piece, :] = kw
        coef[3, piece, :] = kn
        coef[4, piece, :] = ks

    flat = (nplane, LANES)
    lane_f = lanes_of(flat)
    plane_f = rows_of(flat)

    def spread(value):
        return jnp.concatenate([value] * nfield, axis=0)

    for which, buf, row, inner in ((0, srows, low_row, PAD), (1, nrows, top_row, top_row - 1)):
        for p in range(nplane):
            edge_rows[pl.ds(p, 1), :] = ext0[p, pl.ds(inner, 1), :]
        x, outer, within = buf[pl.ds(0, nplane), :], buf[pl.ds(32, nplane), :], edge_rows[...]
        south, north = (outer, within) if which == 0 else (within, outer)
        ends = jnp.broadcast_to(halo0[pl.ds(row, 1), :], flat)
        at_west = jnp.sum(jnp.where(lane_f == 4 * plane_f + 1, ends, 0.0), axis=1, keepdims=True)
        at_east = jnp.sum(jnp.where(lane_f == 4 * plane_f, ends, 0.0), axis=1, keepdims=True)
        left = jnp.where(lane_f == 0, at_west, roll(x, 1, 1))
        right = jnp.where(lane_f == LANES - 1, at_east, roll(x, -1, 1))
        raw = buf[pl.ds(nplane, 1), :]
        n_near = buf[pl.ds(nplane + 1, 1), :]
        n_far = buf[pl.ds(32 + nplane + 1, 1), :]
        k = buf[pl.ds(nplane + 2, 1), :]
        one = (1, LANES)
        lane_1 = lanes_of(one)
        w_end = roll(strips[0, pl.ds(row, 1), :], -(4 * nplane + 1), 1)
        e_end = roll(strips[1, pl.ds(row, 1), :], LANES - 1 - (4 * nplane + 1), 1)
        if which == 1:
            shifted = roll(raw, -1, 1)
            e_weight = jnp.where(at_top(one), shifted, raw)
        else:
            e_weight = raw
        e_weight = jnp.where(lane_1 == LANES - 1, e_end, e_weight)
        w_weight = jnp.where(lane_1 == 0, w_end, roll(e_weight, 1, 1))
        if which == 0:
            n_north, n_south = n_near, n_far
        else:
            n_north = jnp.where(at_top(one), n_far, n_near)
            n_south = jnp.where(at_top(one), n_near, weights[1, pl.ds(rows - 1, 1), :])
        ke, kw, kn, ks = k * e_weight, k * w_weight, k * n_north, k * n_south
        base = 1.0 - ((ke + kw) + (kn + ks))
        at_u, at_v = slice(4 * nlevel, 5 * nlevel), slice(5 * nlevel, 6 * nlevel)
        c = coefficients(
            base, ke, kw, kn, ks,
            spread(x[at_u]), spread(left[at_u]), spread(right[at_u]),
            spread(x[at_v]), spread(south[at_v]), spread(north[at_v]),
        )
        edge_rows[...] = stencil(c, x, left, right, south, north)
        for p in range(nplane):
            ext1[p, pl.ds(row, 1), :] = edge_rows[pl.ds(p, 1), :]

    def advance(source, halo, level, put):
        for start in range(0, rows, CHUNK):
            piece = pl.ds(start, CHUNK)
            base, ke, kw, kn, ks = (coef[i, piece, :] for i in range(5))
            ends = halo[pl.ds(PAD + start, CHUNK), :]

            def centre(field):
                return source[field * nlevel + level, pl.ds(PAD + start, CHUNK), :]

            def sides(field, x):
                end = pltpu.roll(ends, LANES - 1 - 4 * (field * nlevel + level), 1)
                return (
                    jnp.where(lane_c == 0, end, roll(x, 1, 1)),
                    jnp.where(lane_c == LANES - 1, end, roll(x, -1, 1)),
                )

            def rows_beside(field):
                return (
                    source[field * nlevel + level, pl.ds(PAD + start - 1, CHUNK), :],
                    source[field * nlevel + level, pl.ds(PAD + start + 1, CHUNK), :],
                )

            u, v = centre(4), centre(5)
            u_sides, v_sides = sides(4, u), rows_beside(5)
            c = coefficients(base, ke, kw, kn, ks, u, *u_sides, v, *v_sides)
            for field in range(nfield):
                x = centre(field)
                left, right = u_sides if field == 4 else sides(field, x)
                south, north = v_sides if field == 5 else rows_beside(field)
                put(field, start, stencil(c, x, left, right, south, north))

    @pl.loop(0, nlevel)
    def _(level):
        def put(field, start, value):
            ext1[field * nlevel + level, pl.ds(PAD + start, CHUNK), :] = value

        advance(ext0, halo0, level, put)

    def store(level):
        return pltpu.make_async_copy(obuf.at[level], out.at[:, level], out_sems.at[level])

    @pl.loop(0, nlevel)
    def _(level):
        def put(field, start, value):
            obuf[level, field, pl.ds(start, CHUNK), :] = value

        advance(ext1, halo1, level, put)
        store(level).start()

    for level in range(nlevel):
        store(level).wait()


def solution(mesh):
    nlon, nlat = mesh.shape["lon"], mesh.shape["lat"]

    def local(fields, face_weights, inv_area, cell_mask, land_blocks):
        nfield, nlevel, rows, cols = fields.shape
        nplane = nfield * nlevel
        tall = rows + 2 * PAD
        f32 = jnp.float32
        anywhere = pl.BlockSpec(memory_space=pl.ANY)

        def body(*refs):
            kernel(nlon, nlat, nfield, nlevel, *refs)

        return pl.pallas_call(
            body,
            out_shape=jax.ShapeDtypeStruct(fields.shape, f32),
            in_specs=[anywhere] * 4 + [pl.BlockSpec(memory_space=pltpu.SMEM)],
            out_specs=anywhere,
            scratch_shapes=[
                pltpu.VMEM((nplane, tall, cols), f32),
                pltpu.VMEM((nplane, tall, cols), f32),
                pltpu.VMEM((nlevel, nfield, rows, cols), f32),
                pltpu.VMEM((2, rows, cols), f32),
                pltpu.VMEM((rows, cols), f32),
                pltpu.VMEM((rows, cols), jnp.int32),
                pltpu.VMEM((rows, cols), f32),
                pltpu.VMEM((rows, cols), f32),
                pltpu.VMEM((72, cols), f32),
                pltpu.VMEM((72, cols), f32),
                pltpu.VMEM((2, rows, cols), f32),
                pltpu.VMEM((2, 72, cols), f32),
                pltpu.VMEM((4, 8, cols), f32),
                pltpu.VMEM((tall, cols), f32),
                pltpu.VMEM((tall, cols), f32),
                pltpu.VMEM((5, rows, cols), f32),
                pltpu.VMEM((2, tall, cols), f32),
                pltpu.VMEM((64, cols), f32),
                pltpu.VMEM((64, cols), f32),
                pltpu.VMEM((nplane, cols), f32),
                pltpu.SemaphoreType.DMA((4,)),
                pltpu.SemaphoreType.DMA((nlevel,)),
                pltpu.SemaphoreType.DMA((8,)),
                pltpu.SemaphoreType.DMA((8,)),
            ],
            compiler_params=pltpu.CompilerParams(
                collective_id=0, has_side_effects=True, vmem_limit_bytes=32 * 1024 * 1024
            ),
        )(fields.reshape(nplane, rows, cols), face_weights, inv_area, cell_mask, land_blocks)

    in_specs = (
        P(None, None, "lat", "lon"),
        P(None, "lat", "lon"),
        P("lat", "lon"),
        P("lat", "lon"),
        P("lat", "lon"),
    )
    out_specs = P(None, None, "lat", "lon")
    return jax.shard_map(local, mesh=mesh, in_specs=in_specs, out_specs=out_specs, check_vma=False)
```

time: 74.7 us -> 20.5 us (0.27)
  the two profiles are of different devices: /device:TPU:12 before, /device:TPU:1 now
where the time goes in v1:
time: 20.5 us; the launch traced here: 20.2 us
  Pallas kernels  14.4 us (70%)
  local copies, waits for them, and re-layouts  5.13 us (25%)
  between operations  0.67 us (3%)
    pallas_call x1, Pallas kernels, local(): pl.pallas_call(body, out_shape=jax.ShapeDtypeStruct(fields.shape, f32), i...  14.4 us
    unnamed x9, local copies, waits for them, and re-layouts  5.13 us

profile of v1, /device:TPU:1, one launch (start us, length us, event | category | flops | bytes accessed | tf_op | source)
XLA Modules:
  0.0 20.2 jit_solution(1130461053201775935)
XLA Ops:
  0.7 0.0 copy-start
  0.7 1.4 %copy-done = f32[6,4,128,128]{3,2,1,0:T(8,128)S(1)} copy-done((f32[6,4,128,128]{3,2,1,0:T(8,128)S(1)}, f32[6,4,128,128]{3,2,1,0:T(8,128)}, u32[]{:S(2)}) %copy-start) | copy-done | bytes 1572888
  2.1 0.0 copy-start.1
  2.1 0.9 %copy-done.1 = f32[2,128,128]{2,1,0:T(8,128)S(1)} copy-done((f32[2,128,128]{2,1,0:T(8,128)S(1)}, f32[2,128,128]{2,1,0:T(8,128)}, u32[]{:S(2)}) %copy-start.1) | copy-done | bytes 131096
  3.0 0.0 copy-start.2
  3.0 0.8 %copy-done.2 = f32[128,128]{1,0:T(8,128)S(1)} copy-done((f32[128,128]{1,0:T(8,128)S(1)}, f32[128,128]{1,0:T(8,128)}, u32[]{:S(2)}) %copy-start.2) | copy-done | bytes 65560
  3.8 0.0 copy-start.3
  3.8 0.8 %copy-done.3 = s32[128,128]{1,0:T(8,128)S(1)} copy-done((s32[128,128]{1,0:T(8,128)S(1)}, s32[128,128]{1,0:T(8,128)}, u32[]{:S(2)}) %copy-start.3) | copy-done | bytes 65560
  4.6 14.4 %shard_map.55 = f32[6,4,128,128]{3,2,1,0:T(8,128)S(1)} custom-call(f32[24,128,128]{2,1,0:T(8,128)S(1)} %bitcast.1, f32[2,128,128]{2,1,0:T(8,128)S(1)} %copy-done.1, f32[128,128]{1,0:T(8,128)S(1)} %copy-done.2, s32[128,128]{1,0:T(8,128)S(1)} %copy-done.3, s32[1,1]{1,0:T(1,128)S(6)} %copy.7.refs_4_), custom_call_target="tpu_custom_call" | custom-call | tf_op jit(solution)/shard_map/pallas_call | solution.py:439
  19.1 1.1 %copy.8 = f32[6,4,128,128]{3,2,1,0:T(8,128)} copy(f32[6,4,128,128]{3,2,1,0:T(8,128)S(1)} %shard_map.55) | data formatting | bytes 3145728
Async XLA Ops:
  0.7 1.4 %copy-start = (f32[6,4,128,128]{3,2,1,0:T(8,128)S(1)}, f32[6,4,128,128]{3,2,1,0:T(8,128)}, u32[]{:S(2)}) copy-start(f32[6,4,128,128]{3,2,1,0:T(8,128)} %param.5) | copy-start | bytes 4718596
  2.1 0.9 %copy-start.1 = (f32[2,128,128]{2,1,0:T(8,128)S(1)}, f32[2,128,128]{2,1,0:T(8,128)}, u32[]{:S(2)}) copy-start(f32[2,128,128]{2,1,0:T(8,128)} %refs_1_.1) | copy-start | bytes 393220
  3.0 0.8 %copy-start.2 = (f32[128,128]{1,0:T(8,128)S(1)}, f32[128,128]{1,0:T(8,128)}, u32[]{:S(2)}) copy-start(f32[128,128]{1,0:T(8,128)} %refs_2_.1) | copy-start | bytes 196612
  3.8 0.8 %copy-start.3 = (s32[128,128]{1,0:T(8,128)S(1)}, s32[128,128]{1,0:T(8,128)}, u32[]{:S(2)}) copy-start(s32[128,128]{1,0:T(8,128)} %refs_3_.1) | copy-start | bytes 196612

commit v2 on v1

--- a/solution.py
+++ b/solution.py
@@ -41,13 +41,47 @@
     return base + ((pw - pe) + (ps - pn)), ke - pe, kw + pw, kn - pn, ks + ps
 
 
-def kernel(
+def advance(source, halo, coef, nfield, nlevel, level, put):
+    rows = coef.shape[1]
+    lane_c = lanes_of((CHUNK, LANES))
+    for start in range(0, rows, CHUNK):
+        piece = pl.ds(start, CHUNK)
+        base, ke, kw, kn, ks = (coef[i, piece, :] for i in range(5))
+        ends = halo[pl.ds(PAD + start, CHUNK), :]
+
+        def centre(field):
+            return source[field * nlevel + level, pl.ds(PAD + start, CHUNK), :]
+
+        def sides(field, x):
+            end = pltpu.roll(ends, LANES - 1 - 4 * (field * nlevel + level), 1)
+            return (
+                jnp.where(lane_c == 0, end, roll(x, 1, 1)),
+                jnp.where(lane_c == LANES - 1, end, roll(x, -1, 1)),
+            )
+
+        def rows_beside(field):
+            return (
+                source[field * nlevel + level, pl.ds(PAD + start - 1, CHUNK), :],
+                source[field * nlevel + level, pl.ds(PAD + start + 1, CHUNK), :],
+            )
+
+        u, v = centre(4), centre(5)
+        u_sides, v_sides = sides(4, u), rows_beside(5)
+        c = coefficients(base, ke, kw, kn, ks, u, *u_sides, v, *v_sides)
+        for field in range(nfield):
+            x = centre(field)
+            left, right = u_sides if field == 4 else sides(field, x)
+            south, north = v_sides if field == 5 else rows_beside(field)
+            put(field, start, stencil(c, x, left, right, south, north))
+
+
+def first_kernel(
     nlon, nlat, nfield, nlevel,
     fields, face_weights, inv_area, cell_mask, land,
-    out,
-    ext0, ext1, obuf, weights, area, cells, scale, packed, send_s, send_n,
-    recv_we, recv_ns, recv_c, halo0, halo1, coef, strips, nrows, srows, edge_rows,
-    in_sems, out_sems, send_sems, recv_sems,
+    ext1, halo1, coef,
+    ext0, weights, area, cells, scale, packed, send_s, send_n,
+    recv_we, recv_ns, recv_c, halo0, strips, nrows, srows, edge_rows,
+    in_sems, send_sems, recv_sems,
 ):
     nplane = nfield * nlevel
     rows = ext0.shape[1] - 2 * PAD
@@ -370,44 +404,15 @@
         for p in range(nplane):
             ext1[p, pl.ds(row, 1), :] = edge_rows[pl.ds(p, 1), :]
 
-    def advance(source, halo, level, put):
-        for start in range(0, rows, CHUNK):
-            piece = pl.ds(start, CHUNK)
-            base, ke, kw, kn, ks = (coef[i, piece, :] for i in range(5))
-            ends = halo[pl.ds(PAD + start, CHUNK), :]
-
-            def centre(field):
-                return source[field * nlevel + level, pl.ds(PAD + start, CHUNK), :]
-
-            def sides(field, x):
-                end = pltpu.roll(ends, LANES - 1 - 4 * (field * nlevel + level), 1)
-                return (
-                    jnp.where(lane_c == 0, end, roll(x, 1, 1)),
-                    jnp.where(lane_c == LANES - 1, end, roll(x, -1, 1)),
-                )
-
-            def rows_beside(field):
-                return (
-                    source[field * nlevel + level, pl.ds(PAD + start - 1, CHUNK), :],
-                    source[field * nlevel + level, pl.ds(PAD + start + 1, CHUNK), :],
-                )
-
-            u, v = centre(4), centre(5)
-            u_sides, v_sides = sides(4, u), rows_beside(5)
-            c = coefficients(base, ke, kw, kn, ks, u, *u_sides, v, *v_sides)
-            for field in range(nfield):
-                x = centre(field)
-                left, right = u_sides if field == 4 else sides(field, x)
-                south, north = v_sides if field == 5 else rows_beside(field)
-                put(field, start, stencil(c, x, left, right, south, north))
-
     @pl.loop(0, nlevel)
     def _(level):
         def put(field, start, value):
             ext1[field * nlevel + level, pl.ds(PAD + start, CHUNK), :] = value
 
-        advance(ext0, halo0, level, put)
-
+        advance(ext0, halo0, coef, nfield, nlevel, level, put)
+
+
+def second_kernel(nfield, nlevel, ext1, halo1, coef, out, obuf, out_sems):
     def store(level):
         return pltpu.make_async_copy(obuf.at[level], out.at[:, level], out_sems.at[level])
 
@@ -416,7 +421,7 @@
         def put(field, start, value):
             obuf[level, field, pl.ds(start, CHUNK), :] = value
 
-        advance(ext1, halo1, level, put)
+        advance(ext1, halo1, coef, nfield, nlevel, level, put)
         store(level).start()
 
     for level in range(nlevel):
@@ -432,19 +437,28 @@
         tall = rows + 2 * PAD
         f32 = jnp.float32
         anywhere = pl.BlockSpec(memory_space=pl.ANY)
-
-        def body(*refs):
-            kernel(nlon, nlat, nfield, nlevel, *refs)
-
-        return pl.pallas_call(
-            body,
-            out_shape=jax.ShapeDtypeStruct(fields.shape, f32),
+        near = pl.BlockSpec(memory_space=pltpu.VMEM)
+
+        def far(value):
+            return pltpu.with_memory_space_constraint(value, pltpu.HBM)
+
+        def first(*refs):
+            first_kernel(nlon, nlat, nfield, nlevel, *refs)
+
+        def second(*refs):
+            second_kernel(nfield, nlevel, *refs)
+
+        passed = pl.pallas_call(
+            first,
+            out_shape=[
+                pltpu.VMEM((nplane, tall, cols), f32),
+                pltpu.VMEM((tall, cols), f32),
+                pltpu.VMEM((5, rows, cols), f32),
+            ],
             in_specs=[anywhere] * 4 + [pl.BlockSpec(memory_space=pltpu.SMEM)],
-            out_specs=anywhere,
+            out_specs=[near] * 3,
             scratch_shapes=[
                 pltpu.VMEM((nplane, tall, cols), f32),
-                pltpu.VMEM((nplane, tall, cols), f32),
-                pltpu.VMEM((nlevel, nfield, rows, cols), f32),
                 pltpu.VMEM((2, rows, cols), f32),
                 pltpu.VMEM((rows, cols), f32),
                 pltpu.VMEM((rows, cols), jnp.int32),
@@ -456,21 +470,32 @@
                 pltpu.VMEM((2, 72, cols), f32),
                 pltpu.VMEM((4, 8, cols), f32),
                 pltpu.VMEM((tall, cols), f32),
-                pltpu.VMEM((tall, cols), f32),
-                pltpu.VMEM((5, rows, cols), f32),
                 pltpu.VMEM((2, tall, cols), f32),
                 pltpu.VMEM((64, cols), f32),
                 pltpu.VMEM((64, cols), f32),
                 pltpu.VMEM((nplane, cols), f32),
                 pltpu.SemaphoreType.DMA((4,)),
-                pltpu.SemaphoreType.DMA((nlevel,)),
                 pltpu.SemaphoreType.DMA((8,)),
                 pltpu.SemaphoreType.DMA((8,)),
             ],
             compiler_params=pltpu.CompilerParams(
-                collective_id=0, has_side_effects=True, vmem_limit_bytes=32 * 1024 * 1024
+                collective_id=0, has_side_effects=True, vmem_limit_bytes=16 * 1024 * 1024
             ),
-        )(fields.reshape(nplane, rows, cols), face_weights, inv_area, cell_mask, land_blocks)
+        )(
+            far(fields.reshape(nplane, rows, cols)), far(face_weights), far(inv_area),
+            far(cell_mask), land_blocks,
+        )
+        return pl.pallas_call(
+            second,
+            out_shape=pltpu.HBM(fields.shape, f32),
+            in_specs=[near] * 3,
+            out_specs=anywhere,
+            scratch_shapes=[
+                pltpu.VMEM((nlevel, nfield, rows, cols), f32),
+                pltpu.SemaphoreType.DMA((nlevel,)),
+            ],
+            compiler_params=pltpu.CompilerParams(vmem_limit_bytes=16 * 1024 * 1024),
+        )(*(pltpu.with_memory_space_constraint(value, pltpu.VMEM) for value in passed))
 
     in_specs = (
         P(None, None, "lat", "lon"),

time: 20.5 us -> 16.7 us (0.81)
  local copies, waits for them, and re-layouts: 5.13 us -> 0 us
  Pallas kernels: 14.4 us -> 15.9 us
    unnamed x9 -> x0, local copies, waits for them, and re-layouts: 5.13 us -> none
    pallas_call x1 -> x2, Pallas kernels: 14.4 us -> 15.9 us  [the longest x1 13.6 us: local(): pl.pallas_call(first, out_shape=[pltpu.VMEM((nplane, tall, cols), f32), p...]
where the time goes in v2:
time: 16.7 us; the launch traced here: 16.6 us
  Pallas kernels  15.9 us (95%)
  between operations  0.66 us (4%)
    pallas_call x1, Pallas kernels, local(): pl.pallas_call(first, out_shape=[pltpu.VMEM((nplane, tall, cols), f32), p...  13.6 us
    pallas_call x1, Pallas kernels, local(): pl.pallas_call(second, out_shape=pltpu.HBM(fields.shape, f32), in_specs=[...  2.33 us

profile of v2, /device:TPU:1, one launch (start us, length us, event | category | flops | bytes accessed | tf_op | source)
XLA Modules:
  0.0 16.6 jit_solution(99461449179167033)
XLA Ops:
  0.7 13.6 %shard_map.55 = (f32[24,144,128]{2,1,0:T(8,128)S(1)}, f32[144,128]{1,0:T(8,128)S(1)}, f32[5,128,128]{2,1,0:T(8,128)S(1)}) custom-call(f32[24,128,128]{2,1,0:T(8,128)} %bitcast.1, f32[2,128,128]{2,1,0:T(8,128)} %refs_1_.1, f32[128,128]{1,0:T(8,128)} %refs_2_.1, s32[128,128]{1,0:T(8,128)} %refs_3_.1, s32[1,1]{1,0:T(1,128)S(6)} %copy.6.refs_4_), custom_call_target="tpu_custom_call" | custom-call | tf_op jit(solution)/shard_map/pallas_call | solution.py:451
  14.2 2.3 %shard_map.56 = f32[6,4,128,128]{3,2,1,0:T(8,128)} custom-call(f32[24,144,128]{2,1,0:T(8,128)S(1)} %get-tuple-element.8.refs_0_, f32[144,128]{1,0:T(8,128)S(1)} %get-tuple-element.9.refs_1_, f32[5,128,128]{2,1,0:T(8,128)S(1)} %get-tuple-element.10.refs_2_), custom_call_target="tpu_custom_call" | custom-call | tf_op jit(solution)/shard_map/pallas_call | solution.py:488

commit v3 on v2

--- a/solution.py
+++ b/solution.py
@@ -47,12 +47,14 @@
     for start in range(0, rows, CHUNK):
         piece = pl.ds(start, CHUNK)
         base, ke, kw, kn, ks = (coef[i, piece, :] for i in range(5))
-        ends = halo[pl.ds(PAD + start, CHUNK), :]
+        ends = None if halo is None else halo[pl.ds(PAD + start, CHUNK), :]
 
         def centre(field):
             return source[field * nlevel + level, pl.ds(PAD + start, CHUNK), :]
 
         def sides(field, x):
+            if ends is None:
+                return roll(x, 1, 1), roll(x, -1, 1)
             end = pltpu.roll(ends, LANES - 1 - 4 * (field * nlevel + level), 1)
             return (
                 jnp.where(lane_c == 0, end, roll(x, 1, 1)),
@@ -80,7 +82,7 @@
     fields, face_weights, inv_area, cell_mask, land,
     ext1, halo1, coef,
     ext0, weights, area, cells, scale, packed, send_s, send_n,
-    recv_we, recv_ns, recv_c, halo0, strips, nrows, srows, edge_rows,
+    send_we, recv_we, recv_ns, recv_c, edges, strips, nrows, srows, edge_rows,
     in_sems, send_sems, recv_sems,
 ):
     nplane = nfield * nlevel
@@ -126,23 +128,30 @@
         greet(east, lat - 1)
         greet(west, lat - 1)
 
+    starts = range(0, rows, CHUNK)
     loads = [
-        pltpu.make_async_copy(fields, ext0.at[:, pl.ds(PAD, rows), :], in_sems.at[0]),
-        pltpu.make_async_copy(face_weights, weights, in_sems.at[1]),
-        pltpu.make_async_copy(inv_area, area, in_sems.at[2]),
-        pltpu.make_async_copy(cell_mask, cells, in_sems.at[3]),
+        pltpu.make_async_copy(face_weights, weights, in_sems.at[0]),
+        pltpu.make_async_copy(inv_area, area, in_sems.at[1]),
+        pltpu.make_async_copy(cell_mask, cells, in_sems.at[2]),
     ]
+    pieces = [
+        pltpu.make_async_copy(
+            fields.at[:, pl.ds(start, CHUNK), :], ext0.at[:, pl.ds(PAD + start, CHUNK), :],
+            in_sems.at[3 + i],
+        )
+        for i, start in enumerate(starts)
+    ]
+    for load in loads + pieces:
+        load.start()
     for load in loads:
-        load.start()
-    for load in loads[1:]:
         load.wait()
     sea = (1 - land[0, 0]).astype(jnp.float32)
     scale[...] = (TIME_STEP * sea) * cells[...].astype(jnp.float32) * area[...]
-    loads[0].wait()
 
     group = lanes_of((CHUNK, LANES)) // 4
-    for start in range(0, rows, CHUNK):
+    for start, load in zip(starts, pieces):
         piece = pl.ds(start, CHUNK)
+        load.wait()
         gathered = jnp.zeros((CHUNK, LANES), jnp.float32)
         for p in range(nplane + 3):
             if p < nplane:
@@ -153,6 +162,15 @@
                 plane = scale[piece, :]
             gathered = jnp.where(group == p, roll(plane, 4 * p + 2, 1), gathered)
         packed[piece, :] = gathered
+    half = rows // 2
+    lane_h = lanes_of((half, LANES))
+    pick = 4 * ((lane_h % 64) // 2) + lane_h % 2
+    for side in range(2):
+        send_we[side] = jnp.where(
+            lane_h < 64,
+            take_lanes(packed[pl.ds(0, half), :], pick + 2 * side),
+            take_lanes(packed[pl.ds(half, half), :], pick + 2 * side),
+        )
     for buf, first, second, corner in ((send_s, 0, 1, 0), (send_n, rows - 1, rows - 2, rows - 8)):
         for at, row in ((0, first), (32, second)):
             for p in range(nplane):
@@ -170,8 +188,8 @@
         )
 
     corner_s, corner_n = send_s.at[pl.ds(64, 8), :], send_n.at[pl.ds(64, 8), :]
-    go_w = remote(packed, recv_we.at[1], 0, EAST, west, lat)
-    go_e = remote(packed, recv_we.at[0], 1, WEST, east, lat)
+    go_w = remote(send_we.at[1], recv_we.at[1], 0, EAST, west, lat)
+    go_e = remote(send_we.at[0], recv_we.at[0], 1, WEST, east, lat)
     go_n = remote(
         send_n, recv_ns.at[jnp.where(is_top, 1, 0)], 2,
         jnp.where(is_top, NORTH, SOUTH), north_lon, north_lat,
@@ -222,6 +240,41 @@
         recv_c[0] = jnp.zeros(recv_c.shape[1:], jnp.float32)
         recv_c[1] = jnp.zeros(recv_c.shape[1:], jnp.float32)
 
+    def set_coefficients(complete):
+        lane_c = lanes_of((CHUNK, LANES))
+        for start in starts:
+            piece = pl.ds(start, CHUNK)
+            k = scale[piece, :]
+            e_weight = weights[0, piece, :]
+            n_weight = weights[1, piece, :]
+            w_weight = roll(e_weight, 1, 1)
+            if complete:
+                outer = roll(strips[0, pl.ds(PAD + start, CHUNK), :], -(4 * nplane + 1), 1)
+                w_weight = jnp.where(lane_c == 0, outer, w_weight)
+            if start:
+                s_weight = weights[1, pl.ds(start - 1, CHUNK), :]
+            else:
+                s_weight = roll(n_weight, 1, 0)
+                if complete:
+                    s_weight = jnp.where(
+                        rows_of((CHUNK, LANES)) == 0, srows[pl.ds(nplane + 1, 1), :], s_weight
+                    )
+            ke, kw, kn, ks = k * e_weight, k * w_weight, k * n_weight, k * s_weight
+            coef[0, piece, :] = 1.0 - ((ke + kw) + (kn + ks))
+            coef[1, piece, :] = ke
+            coef[2, piece, :] = kw
+            coef[3, piece, :] = kn
+            coef[4, piece, :] = ks
+
+    set_coefficients(False)
+
+    @pl.loop(0, nlevel)
+    def _(level):
+        def put(field, start, value):
+            ext1[field * nlevel + level, pl.ds(PAD + start, CHUNK), :] = value
+
+        advance(ext0, None, coef, nfield, nlevel, level, put)
+
     def arrived(dst, slot):
         remote(dst, dst, 0, slot, west, lat).wait_recv()
 
@@ -272,9 +325,6 @@
         at_top(shape), flips * take_lanes(came, LANES - 1 - lanes_of(shape)), came
     )
     srows[...] = recv_ns[0, pl.ds(0, 64), :]
-    for p in range(nplane):
-        ext0[p, pl.ds(top_row, 1), :] = nrows[pl.ds(p, 1), :]
-        ext0[p, pl.ds(low_row, 1), :] = srows[pl.ds(p, 1), :]
 
     eight = (8, LANES)
     lane8 = lanes_of(eight)
@@ -290,9 +340,13 @@
 
     middle_n = recv_ns[1, pl.ds(64, 8), :]
     middle_s = recv_ns[0, pl.ds(64, 8), :]
-    slot = lanes_of((rows, LANES)) % 4
-    strips[0, pl.ds(PAD, rows), :] = jnp.where(slot < 2, recv_we[0], packed[...])
-    strips[1, pl.ds(PAD, rows), :] = jnp.where(slot < 2, packed[...], recv_we[1])
+    slot = lane_h % 4
+    place = 2 * (lane_h // 4) + lane_h % 2
+    for start in (0, half):
+        piece = pl.ds(start, half)
+        own, at = packed[piece, :], place + (64 if start else 0)
+        strips[0, pl.ds(PAD + start, half), :] = jnp.where(slot < 2, take_lanes(recv_we[0], at), own)
+        strips[1, pl.ds(PAD + start, half), :] = jnp.where(slot < 2, own, take_lanes(recv_we[1], at))
     strips[0, pl.ds(0, 8), :] = jnp.where(slot8 < 2, recv_c[0], middle_s)
     strips[1, pl.ds(0, 8), :] = jnp.where(slot8 < 2, middle_s, recv_c[1])
     for side in range(2):
@@ -331,70 +385,21 @@
         advanced.append(
             stencil(c, x, roll(x, 1, 1), roll(x, -1, 1), roll(x, 1, 0), roll(x, -1, 0))
         )
-    halo0[...] = halo_of(strips[0], strips[1])
     halo1[...] = halo_of(advanced[0], advanced[1])
-
-    lane_c = lanes_of((CHUNK, LANES))
-    for start in range(0, rows, CHUNK):
-        piece = pl.ds(start, CHUNK)
-        k = scale[piece, :]
-        e_weight = weights[0, piece, :]
-        n_weight = weights[1, piece, :]
-        outer = roll(strips[0, pl.ds(PAD + start, CHUNK), :], -(4 * nplane + 1), 1)
-        w_weight = jnp.where(lane_c == 0, outer, roll(e_weight, 1, 1))
-        if start:
-            s_weight = weights[1, pl.ds(start - 1, CHUNK), :]
-        else:
-            s_weight = jnp.where(
-                rows_of((CHUNK, LANES)) == 0, srows[pl.ds(nplane + 1, 1), :], roll(n_weight, 1, 0)
-            )
-        ke, kw, kn, ks = k * e_weight, k * w_weight, k * n_weight, k * s_weight
-        coef[0, piece, :] = 1.0 - ((ke + kw) + (kn + ks))
-        coef[1, piece, :] = ke
-        coef[2, piece, :] = kw
-        coef[3, piece, :] = kn
-        coef[4, piece, :] = ks
-
-    flat = (nplane, LANES)
-    lane_f = lanes_of(flat)
-    plane_f = rows_of(flat)
+    edges[...] = roll(jnp.where(slot_t == 1, advanced[1], advanced[0]), -1, 1)
+    set_coefficients(True)
+
+    at_u, at_v = slice(4 * nlevel, 5 * nlevel), slice(5 * nlevel, 6 * nlevel)
+    folded_1 = at_top((1, LANES))
 
     def spread(value):
         return jnp.concatenate([value] * nfield, axis=0)
 
-    for which, buf, row, inner in ((0, srows, low_row, PAD), (1, nrows, top_row, top_row - 1)):
-        for p in range(nplane):
-            edge_rows[pl.ds(p, 1), :] = ext0[p, pl.ds(inner, 1), :]
-        x, outer, within = buf[pl.ds(0, nplane), :], buf[pl.ds(32, nplane), :], edge_rows[...]
-        south, north = (outer, within) if which == 0 else (within, outer)
-        ends = jnp.broadcast_to(halo0[pl.ds(row, 1), :], flat)
-        at_west = jnp.sum(jnp.where(lane_f == 4 * plane_f + 1, ends, 0.0), axis=1, keepdims=True)
-        at_east = jnp.sum(jnp.where(lane_f == 4 * plane_f, ends, 0.0), axis=1, keepdims=True)
-        left = jnp.where(lane_f == 0, at_west, roll(x, 1, 1))
-        right = jnp.where(lane_f == LANES - 1, at_east, roll(x, -1, 1))
-        raw = buf[pl.ds(nplane, 1), :]
-        n_near = buf[pl.ds(nplane + 1, 1), :]
-        n_far = buf[pl.ds(32 + nplane + 1, 1), :]
-        k = buf[pl.ds(nplane + 2, 1), :]
-        one = (1, LANES)
-        lane_1 = lanes_of(one)
-        w_end = roll(strips[0, pl.ds(row, 1), :], -(4 * nplane + 1), 1)
-        e_end = roll(strips[1, pl.ds(row, 1), :], LANES - 1 - (4 * nplane + 1), 1)
-        if which == 1:
-            shifted = roll(raw, -1, 1)
-            e_weight = jnp.where(at_top(one), shifted, raw)
-        else:
-            e_weight = raw
-        e_weight = jnp.where(lane_1 == LANES - 1, e_end, e_weight)
-        w_weight = jnp.where(lane_1 == 0, w_end, roll(e_weight, 1, 1))
-        if which == 0:
-            n_north, n_south = n_near, n_far
-        else:
-            n_north = jnp.where(at_top(one), n_far, n_near)
-            n_south = jnp.where(at_top(one), n_near, weights[1, pl.ds(rows - 1, 1), :])
-        ke, kw, kn, ks = k * e_weight, k * w_weight, k * n_north, k * n_south
+    def set_row(row, x, south, north, k, e_weight, n_south, n_north):
+        left, right = roll(x, 1, 1), roll(x, -1, 1)
+        ke, kw = k * e_weight, k * roll(e_weight, 1, 1)
+        kn, ks = k * n_north, k * n_south
         base = 1.0 - ((ke + kw) + (kn + ks))
-        at_u, at_v = slice(4 * nlevel, 5 * nlevel), slice(5 * nlevel, 6 * nlevel)
         c = coefficients(
             base, ke, kw, kn, ks,
             spread(x[at_u]), spread(left[at_u]), spread(right[at_u]),
@@ -404,12 +409,35 @@
         for p in range(nplane):
             ext1[p, pl.ds(row, 1), :] = edge_rows[pl.ds(p, 1), :]
 
-    @pl.loop(0, nlevel)
-    def _(level):
-        def put(field, start, value):
-            ext1[field * nlevel + level, pl.ds(PAD + start, CHUNK), :] = value
-
-        advance(ext0, halo0, coef, nfield, nlevel, level, put)
+    def own_weights(buf):
+        return buf[pl.ds(nplane + 2, 1), :], buf[pl.ds(nplane, 1), :], buf[pl.ds(nplane + 1, 1), :]
+
+    inside, within = send_s[pl.ds(0, nplane), :], send_s[pl.ds(32, nplane), :]
+    near, far = srows[pl.ds(0, nplane), :], srows[pl.ds(32, nplane), :]
+    k, e_weight, n_weight = own_weights(send_s)
+    k_near, e_near, n_near = own_weights(srows)
+    n_far = srows[pl.ds(32 + nplane + 1, 1), :]
+    set_row(PAD, inside, near, within, k, e_weight, n_near, n_weight)
+    set_row(low_row, near, far, inside, k_near, e_near, n_far, n_near)
+
+    inside, within = send_n[pl.ds(0, nplane), :], send_n[pl.ds(32, nplane), :]
+    near, far = nrows[pl.ds(0, nplane), :], nrows[pl.ds(32, nplane), :]
+    k, e_weight, n_weight = own_weights(send_n)
+    n_within = send_n[pl.ds(32 + nplane + 1, 1), :]
+    k_near, e_near, n_near = own_weights(nrows)
+    e_near = jnp.where(folded_1, roll(e_near, -1, 1), e_near)
+    n_far = nrows[pl.ds(32 + nplane + 1, 1), :]
+    set_row(top_row - 1, inside, within, near, k, e_weight, n_within, n_weight)
+    set_row(
+        top_row, near, inside, far, k_near, e_near,
+        jnp.where(folded_1, n_near, n_weight), jnp.where(folded_1, n_far, n_near),
+    )
+
+    lane_t = lanes_of(tall)
+    is_edge = jnp.logical_or(lane_t == 0, lane_t == LANES - 1)
+    at_edges = edges[...]
+    for p in range(nplane):
+        ext1[p] = jnp.where(is_edge, roll(at_edges, LANES - 1 - 4 * p, 1), ext1[p])
 
 
 def second_kernel(nfield, nlevel, ext1, halo1, coef, out, obuf, out_sems):
@@ -466,7 +494,8 @@
                 pltpu.VMEM((rows, cols), f32),
                 pltpu.VMEM((72, cols), f32),
                 pltpu.VMEM((72, cols), f32),
-                pltpu.VMEM((2, rows, cols), f32),
+                pltpu.VMEM((2, rows // 2, cols), f32),
+                pltpu.VMEM((2, rows // 2, cols), f32),
                 pltpu.VMEM((2, 72, cols), f32),
                 pltpu.VMEM((4, 8, cols), f32),
                 pltpu.VMEM((tall, cols), f32),
@@ -474,7 +503,7 @@
                 pltpu.VMEM((64, cols), f32),
                 pltpu.VMEM((64, cols), f32),
                 pltpu.VMEM((nplane, cols), f32),
-                pltpu.SemaphoreType.DMA((4,)),
+                pltpu.SemaphoreType.DMA((3 + rows // CHUNK,)),
                 pltpu.SemaphoreType.DMA((8,)),
                 pltpu.SemaphoreType.DMA((8,)),
             ],

time: 16.7 us -> 15 us (0.90)
  Pallas kernels: 15.9 us -> 14.2 us
    pallas_call x1, Pallas kernels: 13.6 us -> 11.9 us  [local(): pl.pallas_call(first, out_shape=[pltpu.VMEM((nplane, tall, cols), f32), p...]
where the time goes in v3:
time: 15 us; the launch traced here: 14.9 us
  Pallas kernels  14.2 us (95%)
  between operations  0.66 us (4%)
    pallas_call x1, Pallas kernels, local(): pl.pallas_call(first, out_shape=[pltpu.VMEM((nplane, tall, cols), f32), p...  11.9 us
    pallas_call x1, Pallas kernels, local(): pl.pallas_call(second, out_shape=pltpu.HBM(fields.shape, f32), in_specs=[...  2.33 us

profile of v3, /device:TPU:1, one launch (start us, length us, event | category | flops | bytes accessed | tf_op | source)
XLA Modules:
  0.0 14.9 jit_solution(5247622319564871793)
XLA Ops:
  0.7 11.9 %shard_map.55 = (f32[24,144,128]{2,1,0:T(8,128)S(1)}, f32[144,128]{1,0:T(8,128)S(1)}, f32[5,128,128]{2,1,0:T(8,128)S(1)}) custom-call(f32[24,128,128]{2,1,0:T(8,128)} %bitcast.1, f32[2,128,128]{2,1,0:T(8,128)} %refs_1_.1, f32[128,128]{1,0:T(8,128)} %refs_2_.1, s32[128,128]{1,0:T(8,128)} %refs_3_.1, s32[1,1]{1,0:T(1,128)S(6)} %copy.6.refs_4_), custom_call_target="tpu_custom_call" | custom-call | tf_op jit(solution)/shard_map/pallas_call | solution.py:479
  12.5 2.3 %shard_map.56 = f32[6,4,128,128]{3,2,1,0:T(8,128)} custom-call(f32[24,144,128]{2,1,0:T(8,128)S(1)} %get-tuple-element.8.refs_0_, f32[144,128]{1,0:T(8,128)S(1)} %get-tuple-element.9.refs_1_, f32[5,128,128]{2,1,0:T(8,128)S(1)} %get-tuple-element.10.refs_2_), custom_call_target="tpu_custom_call" | custom-call | tf_op jit(solution)/shard_map/pallas_call | solution.py:517

commit v4 on v3

--- a/solution.py
+++ b/solution.py
@@ -41,25 +41,17 @@
     return base + ((pw - pe) + (ps - pn)), ke - pe, kw + pw, kn - pn, ks + ps
 
 
-def advance(source, halo, coef, nfield, nlevel, level, put):
+def advance(source, coef, nfield, nlevel, level, put):
     rows = coef.shape[1]
-    lane_c = lanes_of((CHUNK, LANES))
     for start in range(0, rows, CHUNK):
         piece = pl.ds(start, CHUNK)
         base, ke, kw, kn, ks = (coef[i, piece, :] for i in range(5))
-        ends = None if halo is None else halo[pl.ds(PAD + start, CHUNK), :]
 
         def centre(field):
             return source[field * nlevel + level, pl.ds(PAD + start, CHUNK), :]
 
-        def sides(field, x):
-            if ends is None:
-                return roll(x, 1, 1), roll(x, -1, 1)
-            end = pltpu.roll(ends, LANES - 1 - 4 * (field * nlevel + level), 1)
-            return (
-                jnp.where(lane_c == 0, end, roll(x, 1, 1)),
-                jnp.where(lane_c == LANES - 1, end, roll(x, -1, 1)),
-            )
+        def columns_beside(x):
+            return roll(x, 1, 1), roll(x, -1, 1)
 
         def rows_beside(field):
             return (
@@ -68,11 +60,11 @@
             )
 
         u, v = centre(4), centre(5)
-        u_sides, v_sides = sides(4, u), rows_beside(5)
+        u_sides, v_sides = columns_beside(u), rows_beside(5)
         c = coefficients(base, ke, kw, kn, ks, u, *u_sides, v, *v_sides)
         for field in range(nfield):
             x = centre(field)
-            left, right = u_sides if field == 4 else sides(field, x)
+            left, right = u_sides if field == 4 else columns_beside(x)
             south, north = v_sides if field == 5 else rows_beside(field)
             put(field, start, stencil(c, x, left, right, south, north))
 
@@ -80,9 +72,9 @@
 def first_kernel(
     nlon, nlat, nfield, nlevel,
     fields, face_weights, inv_area, cell_mask, land,
-    ext1, halo1, coef,
-    ext0, weights, area, cells, scale, packed, send_s, send_n,
-    send_we, recv_we, recv_ns, recv_c, edges, strips, nrows, srows, edge_rows,
+    state, columns,
+    ext0, ext1, coef, weights, area, cells, scale, packed, send_s, send_n,
+    send_we, recv_we, recv_ns, recv_c, inner, strips, nrows, srows, edge_rows,
     in_sems, send_sems, recv_sems,
 ):
     nplane = nfield * nlevel
@@ -240,79 +232,43 @@
         recv_c[0] = jnp.zeros(recv_c.shape[1:], jnp.float32)
         recv_c[1] = jnp.zeros(recv_c.shape[1:], jnp.float32)
 
-    def set_coefficients(complete):
-        lane_c = lanes_of((CHUNK, LANES))
-        for start in starts:
-            piece = pl.ds(start, CHUNK)
-            k = scale[piece, :]
-            e_weight = weights[0, piece, :]
-            n_weight = weights[1, piece, :]
-            w_weight = roll(e_weight, 1, 1)
-            if complete:
-                outer = roll(strips[0, pl.ds(PAD + start, CHUNK), :], -(4 * nplane + 1), 1)
-                w_weight = jnp.where(lane_c == 0, outer, w_weight)
-            if start:
-                s_weight = weights[1, pl.ds(start - 1, CHUNK), :]
-            else:
-                s_weight = roll(n_weight, 1, 0)
-                if complete:
-                    s_weight = jnp.where(
-                        rows_of((CHUNK, LANES)) == 0, srows[pl.ds(nplane + 1, 1), :], s_weight
-                    )
-            ke, kw, kn, ks = k * e_weight, k * w_weight, k * n_weight, k * s_weight
-            coef[0, piece, :] = 1.0 - ((ke + kw) + (kn + ks))
-            coef[1, piece, :] = ke
-            coef[2, piece, :] = kw
-            coef[3, piece, :] = kn
-            coef[4, piece, :] = ks
-
-    set_coefficients(False)
+    def set_coefficients(start, row_before):
+        piece = pl.ds(start, CHUNK)
+        k = scale[piece, :]
+        e_weight = weights[0, piece, :]
+        n_weight = weights[1, piece, :]
+        w_weight = roll(e_weight, 1, 1)
+        if start:
+            s_weight = weights[1, pl.ds(start - 1, CHUNK), :]
+        else:
+            s_weight = roll(n_weight, 1, 0)
+            if row_before is not None:
+                s_weight = jnp.where(rows_of((CHUNK, LANES)) == 0, row_before, s_weight)
+        ke, kw, kn, ks = k * e_weight, k * w_weight, k * n_weight, k * s_weight
+        coef[0, piece, :] = 1.0 - ((ke + kw) + (kn + ks))
+        coef[1, piece, :] = ke
+        coef[2, piece, :] = kw
+        coef[3, piece, :] = kn
+        coef[4, piece, :] = ks
+
+    for start in starts:
+        set_coefficients(start, None)
 
     @pl.loop(0, nlevel)
     def _(level):
         def put(field, start, value):
             ext1[field * nlevel + level, pl.ds(PAD + start, CHUNK), :] = value
 
-        advance(ext0, None, coef, nfield, nlevel, level, put)
+        advance(ext0, coef, nfield, nlevel, level, put)
 
     def arrived(dst, slot):
         remote(dst, dst, 0, slot, west, lat).wait_recv()
 
-    arrived(recv_we.at[0], WEST)
-    arrived(recv_we.at[1], EAST)
     arrived(recv_ns.at[1], NORTH)
 
     @pl.when(not_bottom)
     def _():
         arrived(recv_ns.at[0], SOUTH)
-        arrived(recv_c.at[0], SOUTHWEST)
-        arrived(recv_c.at[1], SOUTHEAST)
-
-    @pl.when(ne_other)
-    def _():
-        arrived(recv_c.at[3], NORTHEAST)
-
-    @pl.when(nw_other)
-    def _():
-        arrived(recv_c.at[2], NORTHWEST)
-
-    go_w.wait_send()
-    go_e.wait_send()
-    go_n.wait_send()
-
-    @pl.when(ne_other)
-    def _():
-        go_ne.wait_send()
-
-    @pl.when(nw_other)
-    def _():
-        go_nw.wait_send()
-
-    @pl.when(not_bottom)
-    def _():
-        go_s.wait_send()
-        go_se.wait_send()
-        go_sw.wait_send()
 
     def at_top(shape):
         return jnp.full(shape, lat, jnp.int32) == nlat - 1
@@ -325,6 +281,85 @@
         at_top(shape), flips * take_lanes(came, LANES - 1 - lanes_of(shape)), came
     )
     srows[...] = recv_ns[0, pl.ds(0, 64), :]
+
+    at_u, at_v = slice(4 * nlevel, 5 * nlevel), slice(5 * nlevel, 6 * nlevel)
+    folded_1 = at_top((1, LANES))
+
+    def spread(value):
+        return jnp.concatenate([value] * nfield, axis=0)
+
+    def set_row(row, x, south, north, k, e_weight, n_south, n_north):
+        left, right = roll(x, 1, 1), roll(x, -1, 1)
+        ke, kw = k * e_weight, k * roll(e_weight, 1, 1)
+        kn, ks = k * n_north, k * n_south
+        base = 1.0 - ((ke + kw) + (kn + ks))
+        c = coefficients(
+            base, ke, kw, kn, ks,
+            spread(x[at_u]), spread(left[at_u]), spread(right[at_u]),
+            spread(x[at_v]), spread(south[at_v]), spread(north[at_v]),
+        )
+        edge_rows[...] = stencil(c, x, left, right, south, north)
+        for p in range(nplane):
+            ext1[p, pl.ds(row, 1), :] = edge_rows[pl.ds(p, 1), :]
+
+    def own_weights(buf):
+        return buf[pl.ds(nplane + 2, 1), :], buf[pl.ds(nplane, 1), :], buf[pl.ds(nplane + 1, 1), :]
+
+    inside, within = send_s[pl.ds(0, nplane), :], send_s[pl.ds(32, nplane), :]
+    near, far = srows[pl.ds(0, nplane), :], srows[pl.ds(32, nplane), :]
+    k, e_weight, n_weight = own_weights(send_s)
+    k_near, e_near, n_near = own_weights(srows)
+    n_far = srows[pl.ds(32 + nplane + 1, 1), :]
+    set_row(PAD, inside, near, within, k, e_weight, n_near, n_weight)
+    set_row(low_row, near, far, inside, k_near, e_near, n_far, n_near)
+
+    inside, within = send_n[pl.ds(0, nplane), :], send_n[pl.ds(32, nplane), :]
+    near, far = nrows[pl.ds(0, nplane), :], nrows[pl.ds(32, nplane), :]
+    k, e_weight, n_weight = own_weights(send_n)
+    n_within = send_n[pl.ds(32 + nplane + 1, 1), :]
+    k_near, e_near, n_near = own_weights(nrows)
+    e_near = jnp.where(folded_1, roll(e_near, -1, 1), e_near)
+    n_far = nrows[pl.ds(32 + nplane + 1, 1), :]
+    set_row(top_row - 1, inside, within, near, k, e_weight, n_within, n_weight)
+    set_row(
+        top_row, near, inside, far, k_near, e_near,
+        jnp.where(folded_1, n_near, n_weight), jnp.where(folded_1, n_far, n_near),
+    )
+
+    set_coefficients(0, srows[pl.ds(nplane + 1, 1), :])
+
+    @pl.loop(0, nlevel)
+    def _(level):
+        def put(field, start, value):
+            state[field * nlevel + level, pl.ds(start, CHUNK), :] = value
+
+        advance(ext1, coef, nfield, nlevel, level, put)
+
+    for start in range(0, rows + 2 * PAD, 48):
+        piece = pl.ds(start, 48)
+        lane = lanes_of((48, LANES))
+        gathered = jnp.zeros((48, LANES), jnp.float32)
+        for p in range(nplane):
+            plane = ext1[p, piece, :]
+            gathered = jnp.where(lane // 2 == 2 * p, roll(plane, 4 * p + 3, 1), gathered)
+            gathered = jnp.where(lane // 2 == 2 * p + 1, roll(plane, 4 * p + 1, 1), gathered)
+        inner[piece, :] = gathered
+
+    arrived(recv_we.at[0], WEST)
+    arrived(recv_we.at[1], EAST)
+
+    @pl.when(not_bottom)
+    def _():
+        arrived(recv_c.at[0], SOUTHWEST)
+        arrived(recv_c.at[1], SOUTHEAST)
+
+    @pl.when(ne_other)
+    def _():
+        arrived(recv_c.at[3], NORTHEAST)
+
+    @pl.when(nw_other)
+    def _():
+        arrived(recv_c.at[2], NORTHWEST)
 
     eight = (8, LANES)
     lane8 = lanes_of(eight)
@@ -362,98 +397,74 @@
     lane_t = lanes_of(tall)
     folded = jnp.logical_and(at_top(tall), rows_of(tall) == top_row)
 
-    def halo_of(west_strip, east_strip):
-        return jnp.where(slot_t == 1, west_strip, roll(east_strip, -2, 1))
+    beyond_125 = take_lanes(weights[0], jnp.full((rows, LANES), LANES - 3, jnp.int32))
+    beyond_125 = jnp.concatenate([beyond_125[:PAD], beyond_125, beyond_125[:PAD]], axis=0)
+    inner_all = inner[...]
+    index_u = 16 * nlevel + lane_t % (4 * nlevel)
+    index_v = 20 * nlevel + lane_t % (4 * nlevel)
+
+    def strip_step(w, x, left, right):
+        south, north = roll(x, 1, 0), roll(x, -1, 0)
+        u = take_lanes(x, index_u), take_lanes(left, index_u), take_lanes(right, index_u)
+        v = take_lanes(x, index_v)
+        c = coefficients(*w, *u, v, roll(v, 1, 0), roll(v, -1, 0))
+        return stencil(c, x, left, right, south, north)
 
     advanced = []
     for side in range(2):
         x = strips[side]
-        u = take_lanes(x, 16 * nlevel + lane_t % (4 * nlevel))
-        v = take_lanes(x, 20 * nlevel + lane_t % (4 * nlevel))
         e_weight, n_weight, k = (
             take_lanes(x, 4 * (nplane + i) + slot_t) for i in range(3)
         )
-        n_behind = roll(n_weight, 1, 0)
-        n_south = jnp.where(folded, n_weight, n_behind)
+        w_weight = jnp.where(slot_t == 0, beyond_125, roll(e_weight, 1, 1))
+        n_south = jnp.where(folded, n_weight, roll(n_weight, 1, 0))
         n_north = jnp.where(folded, roll(n_weight, -1, 0), n_weight)
-        ke, kw, kn, ks = k * e_weight, k * roll(e_weight, 1, 1), k * n_north, k * n_south
-        base = 1.0 - ((ke + kw) + (kn + ks))
-        c = coefficients(
-            base, ke, kw, kn, ks,
-            u, roll(u, 1, 1), roll(u, -1, 1), v, roll(v, 1, 0), roll(v, -1, 0),
-        )
-        advanced.append(
-            stencil(c, x, roll(x, 1, 1), roll(x, -1, 1), roll(x, 1, 0), roll(x, -1, 0))
-        )
-    halo1[...] = halo_of(advanced[0], advanced[1])
-    edges[...] = roll(jnp.where(slot_t == 1, advanced[1], advanced[0]), -1, 1)
-    set_coefficients(True)
-
-    at_u, at_v = slice(4 * nlevel, 5 * nlevel), slice(5 * nlevel, 6 * nlevel)
-    folded_1 = at_top((1, LANES))
-
-    def spread(value):
-        return jnp.concatenate([value] * nfield, axis=0)
-
-    def set_row(row, x, south, north, k, e_weight, n_south, n_north):
-        left, right = roll(x, 1, 1), roll(x, -1, 1)
-        ke, kw = k * e_weight, k * roll(e_weight, 1, 1)
-        kn, ks = k * n_north, k * n_south
-        base = 1.0 - ((ke + kw) + (kn + ks))
-        c = coefficients(
-            base, ke, kw, kn, ks,
-            spread(x[at_u]), spread(left[at_u]), spread(right[at_u]),
-            spread(x[at_v]), spread(south[at_v]), spread(north[at_v]),
-        )
-        edge_rows[...] = stencil(c, x, left, right, south, north)
-        for p in range(nplane):
-            ext1[p, pl.ds(row, 1), :] = edge_rows[pl.ds(p, 1), :]
-
-    def own_weights(buf):
-        return buf[pl.ds(nplane + 2, 1), :], buf[pl.ds(nplane, 1), :], buf[pl.ds(nplane + 1, 1), :]
-
-    inside, within = send_s[pl.ds(0, nplane), :], send_s[pl.ds(32, nplane), :]
-    near, far = srows[pl.ds(0, nplane), :], srows[pl.ds(32, nplane), :]
-    k, e_weight, n_weight = own_weights(send_s)
-    k_near, e_near, n_near = own_weights(srows)
-    n_far = srows[pl.ds(32 + nplane + 1, 1), :]
-    set_row(PAD, inside, near, within, k, e_weight, n_near, n_weight)
-    set_row(low_row, near, far, inside, k_near, e_near, n_far, n_near)
-
-    inside, within = send_n[pl.ds(0, nplane), :], send_n[pl.ds(32, nplane), :]
-    near, far = nrows[pl.ds(0, nplane), :], nrows[pl.ds(32, nplane), :]
-    k, e_weight, n_weight = own_weights(send_n)
-    n_within = send_n[pl.ds(32 + nplane + 1, 1), :]
-    k_near, e_near, n_near = own_weights(nrows)
-    e_near = jnp.where(folded_1, roll(e_near, -1, 1), e_near)
-    n_far = nrows[pl.ds(32 + nplane + 1, 1), :]
-    set_row(top_row - 1, inside, within, near, k, e_weight, n_within, n_weight)
-    set_row(
-        top_row, near, inside, far, k_near, e_near,
-        jnp.where(folded_1, n_near, n_weight), jnp.where(folded_1, n_far, n_near),
-    )
-
-    lane_t = lanes_of(tall)
-    is_edge = jnp.logical_or(lane_t == 0, lane_t == LANES - 1)
-    at_edges = edges[...]
-    for p in range(nplane):
-        ext1[p] = jnp.where(is_edge, roll(at_edges, LANES - 1 - 4 * p, 1), ext1[p])
-
-
-def second_kernel(nfield, nlevel, ext1, halo1, coef, out, obuf, out_sems):
-    def store(level):
-        return pltpu.make_async_copy(obuf.at[level], out.at[:, level], out_sems.at[level])
-
-    @pl.loop(0, nlevel)
-    def _(level):
-        def put(field, start, value):
-            obuf[level, field, pl.ds(start, CHUNK), :] = value
-
-        advance(ext1, halo1, coef, nfield, nlevel, level, put)
-        store(level).start()
-
-    for level in range(nlevel):
-        store(level).wait()
+        ke, kw, kn, ks = k * e_weight, k * w_weight, k * n_north, k * n_south
+        w = (1.0 - ((ke + kw) + (kn + ks)), ke, kw, kn, ks)
+        x = strip_step(w, x, roll(x, 1, 1), roll(x, -1, 1))
+        x = jnp.where(
+            slot_t == 0, roll(inner_all, -1, 1), jnp.where(slot_t == 3, roll(inner_all, 1, 1), x)
+        )
+        left = jnp.where(slot_t == 0, inner_all, roll(x, 1, 1))
+        right = jnp.where(slot_t == 3, inner_all, roll(x, -1, 1))
+        advanced.append(strip_step(w, x, left, right))
+    final = jnp.where(slot_t < 2, advanced[1], advanced[0])
+    columns[...] = final[PAD : PAD + rows, :]
+
+    go_w.wait_send()
+    go_e.wait_send()
+    go_n.wait_send()
+
+    @pl.when(ne_other)
+    def _():
+        go_ne.wait_send()
+
+    @pl.when(nw_other)
+    def _():
+        go_nw.wait_send()
+
+    @pl.when(not_bottom)
+    def _():
+        go_s.wait_send()
+        go_se.wait_send()
+        go_sw.wait_send()
+
+
+def second_kernel(state, columns, out, obuf, out_sems):
+    nplane, rows, cols = state.shape
+    lane = lanes_of((rows, cols))
+    is_edge = jnp.logical_or(lane < 2, lane >= LANES - 2)
+    parts = out_sems.shape[0]
+    size = nplane // parts
+    copies = []
+    for part in range(parts):
+        for p in range(part * size, (part + 1) * size):
+            obuf[p] = jnp.where(is_edge, roll(columns[...], -(4 * p + 2), 1), state[p])
+        piece = pl.ds(part * size, size)
+        copies.append(pltpu.make_async_copy(obuf.at[piece], out.at[piece], out_sems.at[part]))
+        copies[-1].start()
+    for copy in copies:
+        copy.wait()
 
 
 def solution(mesh):
@@ -474,19 +485,20 @@
             first_kernel(nlon, nlat, nfield, nlevel, *refs)
 
         def second(*refs):
-            second_kernel(nfield, nlevel, *refs)
+            second_kernel(*refs)
 
         passed = pl.pallas_call(
             first,
             out_shape=[
-                pltpu.VMEM((nplane, tall, cols), f32),
-                pltpu.VMEM((tall, cols), f32),
-                pltpu.VMEM((5, rows, cols), f32),
+                pltpu.VMEM((nplane, rows, cols), f32),
+                pltpu.VMEM((rows, cols), f32),
             ],
             in_specs=[anywhere] * 4 + [pl.BlockSpec(memory_space=pltpu.SMEM)],
-            out_specs=[near] * 3,
+            out_specs=[near] * 2,
             scratch_shapes=[
                 pltpu.VMEM((nplane, tall, cols), f32),
+                pltpu.VMEM((nplane, tall, cols), f32),
+                pltpu.VMEM((5, rows, cols), f32),
                 pltpu.VMEM((2, rows, cols), f32),
                 pltpu.VMEM((rows, cols), f32),
                 pltpu.VMEM((rows, cols), jnp.int32),
@@ -514,17 +526,18 @@
             far(fields.reshape(nplane, rows, cols)), far(face_weights), far(inv_area),
             far(cell_mask), land_blocks,
         )
-        return pl.pallas_call(
+        result = pl.pallas_call(
             second,
-            out_shape=pltpu.HBM(fields.shape, f32),
-            in_specs=[near] * 3,
+            out_shape=pltpu.HBM((nplane, rows, cols), f32),
+            in_specs=[near] * 2,
             out_specs=anywhere,
             scratch_shapes=[
-                pltpu.VMEM((nlevel, nfield, rows, cols), f32),
-                pltpu.SemaphoreType.DMA((nlevel,)),
+                pltpu.VMEM((nplane, rows, cols), f32),
+                pltpu.SemaphoreType.DMA((4,)),
             ],
             compiler_params=pltpu.CompilerParams(vmem_limit_bytes=16 * 1024 * 1024),
         )(*(pltpu.with_memory_space_constraint(value, pltpu.VMEM) for value in passed))
+        return result.reshape(fields.shape)
 
     in_specs = (
         P(None, None, "lat", "lon"),

time: 15 us -> 15.2 us (1.013)
  no operation moved by 1% of the time
where the time goes in v4:
time: 15.2 us; the launch traced here: 15 us
  Pallas kernels  14.3 us (94%)
  between operations  0.66 us (4%)
    pallas_call x1, Pallas kernels, local(): pl.pallas_call(first, out_shape=[pltpu.VMEM((nplane, rows, cols), f32), p...  13 us
    pallas_call x1, Pallas kernels, local(): pl.pallas_call(second, out_shape=pltpu.HBM((nplane, rows, cols), f32), in...  1.34 us

profile of v4, /device:TPU:1, one launch (start us, length us, event | category | flops | bytes accessed | tf_op | source)
XLA Modules:
  0.0 15.0 jit_solution(14852283143385894763)
XLA Ops:
  0.7 13.0 %shard_map.55 = (f32[24,128,128]{2,1,0:T(8,128)S(1)}, f32[128,128]{1,0:T(8,128)S(1)}) custom-call(f32[24,128,128]{2,1,0:T(8,128)} %bitcast.2, f32[2,128,128]{2,1,0:T(8,128)} %refs_1_.1, f32[128,128]{1,0:T(8,128)} %refs_2_.1, s32[128,128]{1,0:T(8,128)} %refs_3_.1, s32[1,1]{1,0:T(1,128)S(6)} %copy.6.refs_4_), custom_call_target="tpu_custom_call" | custom-call | tf_op jit(solution)/shard_map/pallas_call | solution.py:490
  13.7 1.3 %shard_map.56 = f32[24,128,128]{2,1,0:T(8,128)} custom-call(f32[24,128,128]{2,1,0:T(8,128)S(1)} %get-tuple-element.7.refs_0_, f32[128,128]{1,0:T(8,128)S(1)} %get-tuple-element.8.refs_1_), custom_call_target="tpu_custom_call" | custom-call | tf_op jit(solution)/shard_map/pallas_call | solution.py:529

commit v5 on v4

--- a/solution.py
+++ b/solution.py
@@ -164,14 +164,14 @@
             take_lanes(packed[pl.ds(half, half), :], pick + 2 * side),
         )
     for buf, first, second, corner in ((send_s, 0, 1, 0), (send_n, rows - 1, rows - 2, rows - 8)):
-        for at, row in ((0, first), (32, second)):
+        for at, row in ((0, first), (28, second)):
             for p in range(nplane):
                 buf[pl.ds(at + p, 1), :] = ext0[p, pl.ds(PAD + row, 1), :]
             for i in range(2):
                 buf[pl.ds(at + nplane + i, 1), :] = weights[i, pl.ds(row, 1), :]
             buf[pl.ds(at + nplane + 2, 1), :] = scale[pl.ds(row, 1), :]
-            buf[pl.ds(at + nplane + 3, 5), :] = jnp.zeros((5, LANES), jnp.float32)
-        buf[pl.ds(64, 8), :] = packed[pl.ds(corner, 8), :]
+            buf[pl.ds(at + nplane + 3, 1), :] = jnp.zeros((1, LANES), jnp.float32)
+        buf[pl.ds(56, 8), :] = packed[pl.ds(corner, 8), :]
 
     def remote(src, dst, number, slot, to_lon, to_lat):
         return pltpu.make_async_remote_copy(
@@ -179,7 +179,7 @@
             device_id={"lon": to_lon, "lat": to_lat}, device_id_type=pl.DeviceIdType.MESH,
         )
 
-    corner_s, corner_n = send_s.at[pl.ds(64, 8), :], send_n.at[pl.ds(64, 8), :]
+    corner_s, corner_n = send_s.at[pl.ds(56, 8), :], send_n.at[pl.ds(56, 8), :]
     go_w = remote(send_we.at[1], recv_we.at[1], 0, EAST, west, lat)
     go_e = remote(send_we.at[0], recv_we.at[0], 1, WEST, east, lat)
     go_n = remote(
@@ -200,9 +200,9 @@
 
     greetings = 3 + jnp.where(ne_self, 0, 1) + jnp.where(nw_self, 0, 1) + jnp.where(is_bottom, 0, 3)
     pl.semaphore_wait(barrier, greetings)
+    go_n.start()
     go_w.start()
     go_e.start()
-    go_n.start()
 
     @pl.when(ne_other)
     def _():
@@ -220,11 +220,11 @@
 
     @pl.when(ne_self)
     def _():
-        recv_c[3] = send_n[pl.ds(64, 8), :]
+        recv_c[3] = send_n[pl.ds(56, 8), :]
 
     @pl.when(nw_self)
     def _():
-        recv_c[2] = send_n[pl.ds(64, 8), :]
+        recv_c[2] = send_n[pl.ds(56, 8), :]
 
     @pl.when(is_bottom)
     def _():
@@ -232,7 +232,7 @@
         recv_c[0] = jnp.zeros(recv_c.shape[1:], jnp.float32)
         recv_c[1] = jnp.zeros(recv_c.shape[1:], jnp.float32)
 
-    def set_coefficients(start, row_before):
+    def set_coefficients(start):
         piece = pl.ds(start, CHUNK)
         k = scale[piece, :]
         e_weight = weights[0, piece, :]
@@ -242,8 +242,6 @@
             s_weight = weights[1, pl.ds(start - 1, CHUNK), :]
         else:
             s_weight = roll(n_weight, 1, 0)
-            if row_before is not None:
-                s_weight = jnp.where(rows_of((CHUNK, LANES)) == 0, row_before, s_weight)
         ke, kw, kn, ks = k * e_weight, k * w_weight, k * n_weight, k * s_weight
         coef[0, piece, :] = 1.0 - ((ke + kw) + (kn + ks))
         coef[1, piece, :] = ke
@@ -252,7 +250,7 @@
         coef[4, piece, :] = ks
 
     for start in starts:
-        set_coefficients(start, None)
+        set_coefficients(start)
 
     @pl.loop(0, nlevel)
     def _(level):
@@ -260,73 +258,6 @@
             ext1[field * nlevel + level, pl.ds(PAD + start, CHUNK), :] = value
 
         advance(ext0, coef, nfield, nlevel, level, put)
-
-    def arrived(dst, slot):
-        remote(dst, dst, 0, slot, west, lat).wait_recv()
-
-    arrived(recv_ns.at[1], NORTH)
-
-    @pl.when(not_bottom)
-    def _():
-        arrived(recv_ns.at[0], SOUTH)
-
-    def at_top(shape):
-        return jnp.full(shape, lat, jnp.int32) == nlat - 1
-
-    shape = (64, LANES)
-    came = recv_ns[1, pl.ds(0, 64), :]
-    sub = rows_of(shape) % 32
-    flips = jnp.where(jnp.logical_and(sub >= 4 * nlevel, sub < nplane), -1.0, 1.0)
-    nrows[...] = jnp.where(
-        at_top(shape), flips * take_lanes(came, LANES - 1 - lanes_of(shape)), came
-    )
-    srows[...] = recv_ns[0, pl.ds(0, 64), :]
-
-    at_u, at_v = slice(4 * nlevel, 5 * nlevel), slice(5 * nlevel, 6 * nlevel)
-    folded_1 = at_top((1, LANES))
-
-    def spread(value):
-        return jnp.concatenate([value] * nfield, axis=0)
-
-    def set_row(row, x, south, north, k, e_weight, n_south, n_north):
-        left, right = roll(x, 1, 1), roll(x, -1, 1)
-        ke, kw = k * e_weight, k * roll(e_weight, 1, 1)
-        kn, ks = k * n_north, k * n_south
-        base = 1.0 - ((ke + kw) + (kn + ks))
-        c = coefficients(
-            base, ke, kw, kn, ks,
-            spread(x[at_u]), spread(left[at_u]), spread(right[at_u]),
-            spread(x[at_v]), spread(south[at_v]), spread(north[at_v]),
-        )
-        edge_rows[...] = stencil(c, x, left, right, south, north)
-        for p in range(nplane):
-            ext1[p, pl.ds(row, 1), :] = edge_rows[pl.ds(p, 1), :]
-
-    def own_weights(buf):
-        return buf[pl.ds(nplane + 2, 1), :], buf[pl.ds(nplane, 1), :], buf[pl.ds(nplane + 1, 1), :]
-
-    inside, within = send_s[pl.ds(0, nplane), :], send_s[pl.ds(32, nplane), :]
-    near, far = srows[pl.ds(0, nplane), :], srows[pl.ds(32, nplane), :]
-    k, e_weight, n_weight = own_weights(send_s)
-    k_near, e_near, n_near = own_weights(srows)
-    n_far = srows[pl.ds(32 + nplane + 1, 1), :]
-    set_row(PAD, inside, near, within, k, e_weight, n_near, n_weight)
-    set_row(low_row, near, far, inside, k_near, e_near, n_far, n_near)
-
-    inside, within = send_n[pl.ds(0, nplane), :], send_n[pl.ds(32, nplane), :]
-    near, far = nrows[pl.ds(0, nplane), :], nrows[pl.ds(32, nplane), :]
-    k, e_weight, n_weight = own_weights(send_n)
-    n_within = send_n[pl.ds(32 + nplane + 1, 1), :]
-    k_near, e_near, n_near = own_weights(nrows)
-    e_near = jnp.where(folded_1, roll(e_near, -1, 1), e_near)
-    n_far = nrows[pl.ds(32 + nplane + 1, 1), :]
-    set_row(top_row - 1, inside, within, near, k, e_weight, n_within, n_weight)
-    set_row(
-        top_row, near, inside, far, k_near, e_near,
-        jnp.where(folded_1, n_near, n_weight), jnp.where(folded_1, n_far, n_near),
-    )
-
-    set_coefficients(0, srows[pl.ds(nplane + 1, 1), :])
 
     @pl.loop(0, nlevel)
     def _(level):
@@ -345,6 +276,95 @@
             gathered = jnp.where(lane // 2 == 2 * p + 1, roll(plane, 4 * p + 1, 1), gathered)
         inner[piece, :] = gathered
 
+    for i, row in enumerate((PAD + 1, PAD + 2, top_row - 2, top_row - 3)):
+        for p in range(nplane):
+            edge_rows[i, pl.ds(p, 1), :] = ext1[p, pl.ds(row, 1), :]
+
+    def arrived(dst, slot):
+        remote(dst, dst, 0, slot, west, lat).wait_recv()
+
+    arrived(recv_ns.at[1], NORTH)
+
+    @pl.when(not_bottom)
+    def _():
+        arrived(recv_ns.at[0], SOUTH)
+
+    def at_top(shape):
+        return jnp.full(shape, lat, jnp.int32) == nlat - 1
+
+    shape = (56, LANES)
+    came = recv_ns[1, pl.ds(0, 56), :]
+    sub = rows_of(shape) % 28
+    flips = jnp.where(jnp.logical_and(sub >= 4 * nlevel, sub < nplane), -1.0, 1.0)
+    nrows[...] = jnp.where(
+        at_top(shape), flips * take_lanes(came, LANES - 1 - lanes_of(shape)), came
+    )
+    srows[...] = recv_ns[0, pl.ds(0, 56), :]
+
+    at_u, at_v = slice(4 * nlevel, 5 * nlevel), slice(5 * nlevel, 6 * nlevel)
+    folded_1 = at_top((1, LANES))
+    flat = (nplane, LANES)
+    lane_f = lanes_of(flat)
+    slot_f = lane_f % 4
+    column_f = jnp.where(slot_f < 2, LANES - 3 + slot_f, slot_f - 1)
+
+    def spread(value):
+        return jnp.concatenate([value] * nfield, axis=0)
+
+    def row_step(x, south, north, k, e_weight, n_south, n_north):
+        left, right = roll(x, 1, 1), roll(x, -1, 1)
+        ke, kw = k * e_weight, k * roll(e_weight, 1, 1)
+        kn, ks = k * n_north, k * n_south
+        base = 1.0 - ((ke + kw) + (kn + ks))
+        c = coefficients(
+            base, ke, kw, kn, ks,
+            spread(x[at_u]), spread(left[at_u]), spread(right[at_u]),
+            spread(x[at_v]), spread(south[at_v]), spread(north[at_v]),
+        )
+        return stencil(c, x, left, right, south, north)
+
+    def to_inner(row, value):
+        picked = jnp.where(rows_of(flat) == lane_f // 4, take_lanes(value, column_f), 0.0)
+        inner[pl.ds(row, 1), :] = jnp.sum(picked, axis=0, keepdims=True)
+
+    def two_rows(buf, first):
+        fields_of = buf[pl.ds(first, nplane), :]
+        e_weight, n_weight, k = (buf[pl.ds(first + nplane + i, 1), :] for i in range(3))
+        return fields_of, k, e_weight, n_weight
+
+    x0, k0, e0, n0 = two_rows(send_s, 0)
+    x1, k1, e1, n1 = two_rows(send_s, 28)
+    y0, ky, ey, ny = two_rows(srows, 0)
+    y1, _, _, ny1 = two_rows(srows, 28)
+    out0 = row_step(y0, y1, x0, ky, ey, ny1, ny)
+    in0 = row_step(x0, y0, x1, k0, e0, ny, n0)
+    in1, in2 = edge_rows[0], edge_rows[1]
+    to_inner(low_row, out0)
+    to_inner(PAD, in0)
+    south_0 = row_step(in0, out0, in1, k0, e0, ny, n0)
+    south_1 = row_step(in1, in0, in2, k1, e1, n0, n1)
+
+    x0, k0, e0, n0 = two_rows(send_n, 0)
+    x1, k1, e1, n1 = two_rows(send_n, 28)
+    n2 = weights[1, pl.ds(rows - 3, 1), :]
+    y0, ky, ey, ny = two_rows(nrows, 0)
+    y1, _, _, ny1 = two_rows(nrows, 28)
+    ey = jnp.where(folded_1, roll(ey, -1, 1), ey)
+    out0 = row_step(
+        y0, x0, y1, ky, ey, jnp.where(folded_1, ny, n0), jnp.where(folded_1, ny1, ny)
+    )
+    in0 = row_step(x0, x1, y0, k0, e0, n1, n0)
+    in1, in2 = edge_rows[2], edge_rows[3]
+    to_inner(top_row, out0)
+    to_inner(top_row - 1, in0)
+    north_0 = row_step(in0, in1, out0, k0, e0, n1, n0)
+    north_1 = row_step(in1, in2, in0, k1, e1, n2, n1)
+    for i, value in enumerate((south_0, south_1, north_0, north_1)):
+        edge_rows[i] = value
+    for i, row in enumerate((0, 1, rows - 1, rows - 2)):
+        for p in range(nplane):
+            state[p, pl.ds(row, 1), :] = edge_rows[i, pl.ds(p, 1), :]
+
     arrived(recv_we.at[0], WEST)
     arrived(recv_we.at[1], EAST)
 
@@ -373,8 +393,8 @@
         mirrored = jnp.where(east8, roll(mirrored, -1, 1), mirrored)
         return mirrored
 
-    middle_n = recv_ns[1, pl.ds(64, 8), :]
-    middle_s = recv_ns[0, pl.ds(64, 8), :]
+    middle_n = recv_ns[1, pl.ds(56, 8), :]
+    middle_s = recv_ns[0, pl.ds(56, 8), :]
     slot = lane_h % 4
     place = 2 * (lane_h // 4) + lane_h % 2
     for start in (0, half):
@@ -504,17 +524,17 @@
                 pltpu.VMEM((rows, cols), jnp.int32),
                 pltpu.VMEM((rows, cols), f32),
                 pltpu.VMEM((rows, cols), f32),
-                pltpu.VMEM((72, cols), f32),
-                pltpu.VMEM((72, cols), f32),
+                pltpu.VMEM((64, cols), f32),
+                pltpu.VMEM((64, cols), f32),
                 pltpu.VMEM((2, rows // 2, cols), f32),
                 pltpu.VMEM((2, rows // 2, cols), f32),
-                pltpu.VMEM((2, 72, cols), f32),
+                pltpu.VMEM((2, 64, cols), f32),
                 pltpu.VMEM((4, 8, cols), f32),
                 pltpu.VMEM((tall, cols), f32),
                 pltpu.VMEM((2, tall, cols), f32),
-                pltpu.VMEM((64, cols), f32),
-                pltpu.VMEM((64, cols), f32),
-                pltpu.VMEM((nplane, cols), f32),
+                pltpu.VMEM((56, cols), f32),
+                pltpu.VMEM((56, cols), f32),
+                pltpu.VMEM((4, nplane, cols), f32),
                 pltpu.SemaphoreType.DMA((3 + rows // CHUNK,)),
                 pltpu.SemaphoreType.DMA((8,)),
                 pltpu.SemaphoreType.DMA((8,)),
@@ -533,7 +553,7 @@
             out_specs=anywhere,
             scratch_shapes=[
                 pltpu.VMEM((nplane, rows, cols), f32),
-                pltpu.SemaphoreType.DMA((4,)),
+                pltpu.SemaphoreType.DMA((8,)),
             ],
             compiler_params=pltpu.CompilerParams(vmem_limit_bytes=16 * 1024 * 1024),
         )(*(pltpu.with_memory_space_constraint(value, pltpu.VMEM) for value in passed))

time: 15.2 us -> 14 us (0.921)
  Pallas kernels: 14.3 us -> 13.2 us
    pallas_call x1, Pallas kernels: 13 us -> 11.9 us  [local(): pl.pallas_call(first, out_shape=[pltpu.VMEM((nplane, rows, cols), f32), p...]
where the time goes in v5:
time: 14 us; the launch traced here: 13.9 us
  Pallas kernels  13.2 us (94%)
  between operations  0.66 us (5%)
    pallas_call x1, Pallas kernels, local(): pl.pallas_call(first, out_shape=[pltpu.VMEM((nplane, rows, cols), f32), p...  11.9 us
    pallas_call x1, Pallas kernels, local(): pl.pallas_call(second, out_shape=pltpu.HBM((nplane, rows, cols), f32), in...  1.32 us

profile of v5, /device:TPU:1, one launch (start us, length us, event | category | flops | bytes accessed | tf_op | source)
XLA Modules:
  0.0 13.9 jit_solution(355542087805468437)
XLA Ops:
  0.7 11.9 %shard_map.55 = (f32[24,128,128]{2,1,0:T(8,128)S(1)}, f32[128,128]{1,0:T(8,128)S(1)}) custom-call(f32[24,128,128]{2,1,0:T(8,128)} %bitcast.2, f32[2,128,128]{2,1,0:T(8,128)} %refs_1_.1, f32[128,128]{1,0:T(8,128)} %refs_2_.1, s32[128,128]{1,0:T(8,128)} %refs_3_.1, s32[1,1]{1,0:T(1,128)S(6)} %copy.6.refs_4_), custom_call_target="tpu_custom_call" | custom-call | tf_op jit(solution)/shard_map/pallas_call | solution.py:510
  12.6 1.3 %shard_map.56 = f32[24,128,128]{2,1,0:T(8,128)} custom-call(f32[24,128,128]{2,1,0:T(8,128)S(1)} %get-tuple-element.7.refs_0_, f32[128,128]{1,0:T(8,128)S(1)} %get-tuple-element.8.refs_1_), custom_call_target="tpu_custom_call" | custom-call | tf_op jit(solution)/shard_map/pallas_call | solution.py:549

commit v6 on v5

--- a/solution.py
+++ b/solution.py
@@ -163,16 +163,6 @@
             take_lanes(packed[pl.ds(0, half), :], pick + 2 * side),
             take_lanes(packed[pl.ds(half, half), :], pick + 2 * side),
         )
-    for buf, first, second, corner in ((send_s, 0, 1, 0), (send_n, rows - 1, rows - 2, rows - 8)):
-        for at, row in ((0, first), (28, second)):
-            for p in range(nplane):
-                buf[pl.ds(at + p, 1), :] = ext0[p, pl.ds(PAD + row, 1), :]
-            for i in range(2):
-                buf[pl.ds(at + nplane + i, 1), :] = weights[i, pl.ds(row, 1), :]
-            buf[pl.ds(at + nplane + 2, 1), :] = scale[pl.ds(row, 1), :]
-            buf[pl.ds(at + nplane + 3, 1), :] = jnp.zeros((1, LANES), jnp.float32)
-        buf[pl.ds(56, 8), :] = packed[pl.ds(corner, 8), :]
-
     def remote(src, dst, number, slot, to_lon, to_lat):
         return pltpu.make_async_remote_copy(
             src_ref=src, dst_ref=dst, send_sem=send_sems.at[number], recv_sem=recv_sems.at[slot],
@@ -200,9 +190,19 @@
 
     greetings = 3 + jnp.where(ne_self, 0, 1) + jnp.where(nw_self, 0, 1) + jnp.where(is_bottom, 0, 3)
     pl.semaphore_wait(barrier, greetings)
-    go_n.start()
     go_w.start()
     go_e.start()
+
+    for buf, first, second, corner in ((send_s, 0, 1, 0), (send_n, rows - 1, rows - 2, rows - 8)):
+        for at, row in ((0, first), (28, second)):
+            for p in range(nplane):
+                buf[pl.ds(at + p, 1), :] = ext0[p, pl.ds(PAD + row, 1), :]
+            for i in range(2):
+                buf[pl.ds(at + nplane + i, 1), :] = weights[i, pl.ds(row, 1), :]
+            buf[pl.ds(at + nplane + 2, 1), :] = scale[pl.ds(row, 1), :]
+            buf[pl.ds(at + nplane + 3, 1), :] = jnp.zeros((1, LANES), jnp.float32)
+        buf[pl.ds(56, 8), :] = packed[pl.ds(corner, 8), :]
+    go_n.start()
 
     @pl.when(ne_other)
     def _():
@@ -365,22 +365,6 @@
         for p in range(nplane):
             state[p, pl.ds(row, 1), :] = edge_rows[i, pl.ds(p, 1), :]
 
-    arrived(recv_we.at[0], WEST)
-    arrived(recv_we.at[1], EAST)
-
-    @pl.when(not_bottom)
-    def _():
-        arrived(recv_c.at[0], SOUTHWEST)
-        arrived(recv_c.at[1], SOUTHEAST)
-
-    @pl.when(ne_other)
-    def _():
-        arrived(recv_c.at[3], NORTHEAST)
-
-    @pl.when(nw_other)
-    def _():
-        arrived(recv_c.at[2], NORTHWEST)
-
     eight = (8, LANES)
     lane8 = lanes_of(eight)
     slot8 = lane8 % 4
@@ -392,25 +376,6 @@
         mirrored = flip8 * take_lanes(upside, lane8 - slot8 + (3 - slot8))
         mirrored = jnp.where(east8, roll(mirrored, -1, 1), mirrored)
         return mirrored
-
-    middle_n = recv_ns[1, pl.ds(56, 8), :]
-    middle_s = recv_ns[0, pl.ds(56, 8), :]
-    slot = lane_h % 4
-    place = 2 * (lane_h // 4) + lane_h % 2
-    for start in (0, half):
-        piece = pl.ds(start, half)
-        own, at = packed[piece, :], place + (64 if start else 0)
-        strips[0, pl.ds(PAD + start, half), :] = jnp.where(slot < 2, take_lanes(recv_we[0], at), own)
-        strips[1, pl.ds(PAD + start, half), :] = jnp.where(slot < 2, own, take_lanes(recv_we[1], at))
-    strips[0, pl.ds(0, 8), :] = jnp.where(slot8 < 2, recv_c[0], middle_s)
-    strips[1, pl.ds(0, 8), :] = jnp.where(slot8 < 2, middle_s, recv_c[1])
-    for side in range(2):
-        lower, upper = ((recv_c[2], middle_n), (middle_n, recv_c[3]))[side]
-        strips[side, pl.ds(top_row, 8), :] = jnp.where(
-            at_top(eight),
-            beyond(jnp.where(slot8 >= 2, lower, upper)),
-            jnp.where(slot8 < 2, lower, upper),
-        )
 
     tall = (rows + 2 * PAD, LANES)
     slot_t = lanes_of(tall) % 4
@@ -430,8 +395,37 @@
         c = coefficients(*w, *u, v, roll(v, 1, 0), roll(v, -1, 0))
         return stencil(c, x, left, right, south, north)
 
-    advanced = []
-    for side in range(2):
+    middle_n = recv_ns[1, pl.ds(56, 8), :]
+    middle_s = recv_ns[0, pl.ds(56, 8), :]
+    slot = lane_h % 4
+    place = 2 * (lane_h // 4) + lane_h % 2
+
+    for turn in range(2):
+        side = jnp.where(lon == 0, 1 - turn, turn)
+        corner_other = jnp.where(side == 0, nw_other.astype(jnp.int32), ne_other.astype(jnp.int32))
+        arrived(recv_we.at[side], WEST + side)
+
+        @pl.when(not_bottom)
+        def _():
+            arrived(recv_c.at[side], SOUTHWEST + side)
+
+        @pl.when(corner_other == 1)
+        def _():
+            arrived(recv_c.at[2 + side], NORTHWEST + side)
+
+        block = recv_we[side]
+        for start in (0, half):
+            at = place + (64 if start else 0)
+            strips[side, pl.ds(PAD + start, half), :] = jnp.where(
+                slot // 2 == side, take_lanes(block, at), packed[pl.ds(start, half), :]
+            )
+        strips[side, pl.ds(0, 8), :] = jnp.where(slot8 // 2 == side, recv_c[side], middle_s)
+        corner = recv_c[2 + side]
+        strips[side, pl.ds(top_row, 8), :] = jnp.where(
+            at_top(eight),
+            beyond(jnp.where(slot8 // 2 == 1 - side, corner, middle_n)),
+            jnp.where(slot8 // 2 == side, corner, middle_n),
+        )
         x = strips[side]
         e_weight, n_weight, k = (
             take_lanes(x, 4 * (nplane + i) + slot_t) for i in range(3)
@@ -447,8 +441,8 @@
         )
         left = jnp.where(slot_t == 0, inner_all, roll(x, 1, 1))
         right = jnp.where(slot_t == 3, inner_all, roll(x, -1, 1))
-        advanced.append(strip_step(w, x, left, right))
-    final = jnp.where(slot_t < 2, advanced[1], advanced[0])
+        strips[side] = strip_step(w, x, left, right)
+    final = jnp.where(slot_t < 2, strips[1], strips[0])
     columns[...] = final[PAD : PAD + rows, :]
 
     go_w.wait_send()

time: 14 us -> 14.2 us (1.014)
  Pallas kernels: 13.2 us -> 13.4 us
    pallas_call x1, Pallas kernels: 11.9 us -> 12.1 us  [local(): pl.pallas_call(first, out_shape=[pltpu.VMEM((nplane, rows, cols), f32), p...]
where the time goes in v6:
time: 14.2 us; the launch traced here: 14.1 us
  Pallas kernels  13.4 us (94%)
  between operations  0.66 us (5%)
    pallas_call x1, Pallas kernels, local(): pl.pallas_call(first, out_shape=[pltpu.VMEM((nplane, rows, cols), f32), p...  12.1 us
    pallas_call x1, Pallas kernels, local(): pl.pallas_call(second, out_shape=pltpu.HBM((nplane, rows, cols), f32), in...  1.32 us

profile of v6, /device:TPU:1, one launch (start us, length us, event | category | flops | bytes accessed | tf_op | source)
XLA Modules:
  0.0 14.1 jit_solution(3063103349713039688)
XLA Ops:
  0.7 12.1 %shard_map.55 = (f32[24,128,128]{2,1,0:T(8,128)S(1)}, f32[128,128]{1,0:T(8,128)S(1)}) custom-call(f32[24,128,128]{2,1,0:T(8,128)} %bitcast.2, f32[2,128,128]{2,1,0:T(8,128)} %refs_1_.1, f32[128,128]{1,0:T(8,128)} %refs_2_.1, s32[128,128]{1,0:T(8,128)} %refs_3_.1, s32[1,1]{1,0:T(1,128)S(6)} %copy.6.refs_4_), custom_call_target="tpu_custom_call" | custom-call | tf_op jit(solution)/shard_map/pallas_call | solution.py:504
  12.8 1.3 %shard_map.56 = f32[24,128,128]{2,1,0:T(8,128)} custom-call(f32[24,128,128]{2,1,0:T(8,128)S(1)} %get-tuple-element.7.refs_0_, f32[128,128]{1,0:T(8,128)S(1)} %get-tuple-element.8.refs_1_), custom_call_target="tpu_custom_call" | custom-call | tf_op jit(solution)/shard_map/pallas_call | solution.py:543

commit v7 on v6

--- a/solution.py
+++ b/solution.py
@@ -169,7 +169,7 @@
             device_id={"lon": to_lon, "lat": to_lat}, device_id_type=pl.DeviceIdType.MESH,
         )
 
-    corner_s, corner_n = send_s.at[pl.ds(56, 8), :], send_n.at[pl.ds(56, 8), :]
+    corner_s, corner_n = packed.at[pl.ds(0, 8), :], packed.at[pl.ds(rows - 8, 8), :]
     go_w = remote(send_we.at[1], recv_we.at[1], 0, EAST, west, lat)
     go_e = remote(send_we.at[0], recv_we.at[0], 1, WEST, east, lat)
     go_n = remote(
@@ -188,50 +188,6 @@
     go_se = remote(corner_s, recv_c.at[2], 6, NORTHWEST, east, lat - 1)
     go_sw = remote(corner_s, recv_c.at[3], 7, NORTHEAST, west, lat - 1)
 
-    greetings = 3 + jnp.where(ne_self, 0, 1) + jnp.where(nw_self, 0, 1) + jnp.where(is_bottom, 0, 3)
-    pl.semaphore_wait(barrier, greetings)
-    go_w.start()
-    go_e.start()
-
-    for buf, first, second, corner in ((send_s, 0, 1, 0), (send_n, rows - 1, rows - 2, rows - 8)):
-        for at, row in ((0, first), (28, second)):
-            for p in range(nplane):
-                buf[pl.ds(at + p, 1), :] = ext0[p, pl.ds(PAD + row, 1), :]
-            for i in range(2):
-                buf[pl.ds(at + nplane + i, 1), :] = weights[i, pl.ds(row, 1), :]
-            buf[pl.ds(at + nplane + 2, 1), :] = scale[pl.ds(row, 1), :]
-            buf[pl.ds(at + nplane + 3, 1), :] = jnp.zeros((1, LANES), jnp.float32)
-        buf[pl.ds(56, 8), :] = packed[pl.ds(corner, 8), :]
-    go_n.start()
-
-    @pl.when(ne_other)
-    def _():
-        go_ne.start()
-
-    @pl.when(nw_other)
-    def _():
-        go_nw.start()
-
-    @pl.when(not_bottom)
-    def _():
-        go_s.start()
-        go_se.start()
-        go_sw.start()
-
-    @pl.when(ne_self)
-    def _():
-        recv_c[3] = send_n[pl.ds(56, 8), :]
-
-    @pl.when(nw_self)
-    def _():
-        recv_c[2] = send_n[pl.ds(56, 8), :]
-
-    @pl.when(is_bottom)
-    def _():
-        recv_ns[0] = jnp.zeros(recv_ns.shape[1:], jnp.float32)
-        recv_c[0] = jnp.zeros(recv_c.shape[1:], jnp.float32)
-        recv_c[1] = jnp.zeros(recv_c.shape[1:], jnp.float32)
-
     def set_coefficients(start):
         piece = pl.ds(start, CHUNK)
         k = scale[piece, :]
@@ -249,36 +205,93 @@
         coef[3, piece, :] = kn
         coef[4, piece, :] = ks
 
-    for start in starts:
-        set_coefficients(start)
-
-    @pl.loop(0, nlevel)
-    def _(level):
-        def put(field, start, value):
-            ext1[field * nlevel + level, pl.ds(PAD + start, CHUNK), :] = value
-
-        advance(ext0, coef, nfield, nlevel, level, put)
-
-    @pl.loop(0, nlevel)
-    def _(level):
-        def put(field, start, value):
-            state[field * nlevel + level, pl.ds(start, CHUNK), :] = value
-
-        advance(ext1, coef, nfield, nlevel, level, put)
-
-    for start in range(0, rows + 2 * PAD, 48):
-        piece = pl.ds(start, 48)
-        lane = lanes_of((48, LANES))
-        gathered = jnp.zeros((48, LANES), jnp.float32)
-        for p in range(nplane):
-            plane = ext1[p, piece, :]
-            gathered = jnp.where(lane // 2 == 2 * p, roll(plane, 4 * p + 3, 1), gathered)
-            gathered = jnp.where(lane // 2 == 2 * p + 1, roll(plane, 4 * p + 1, 1), gathered)
-        inner[piece, :] = gathered
-
-    for i, row in enumerate((PAD + 1, PAD + 2, top_row - 2, top_row - 3)):
-        for p in range(nplane):
-            edge_rows[i, pl.ds(p, 1), :] = ext1[p, pl.ds(row, 1), :]
+    def advance_block():
+        for start in starts:
+            set_coefficients(start)
+
+        @pl.loop(0, nlevel)
+        def _(level):
+            def put(field, start, value):
+                ext1[field * nlevel + level, pl.ds(PAD + start, CHUNK), :] = value
+
+            advance(ext0, coef, nfield, nlevel, level, put)
+
+        @pl.loop(0, nlevel)
+        def _(level):
+            def put(field, start, value):
+                state[field * nlevel + level, pl.ds(start, CHUNK), :] = value
+
+            advance(ext1, coef, nfield, nlevel, level, put)
+
+        for start in range(0, rows + 2 * PAD, 48):
+            piece = pl.ds(start, 48)
+            lane = lanes_of((48, LANES))
+            gathered = jnp.zeros((48, LANES), jnp.float32)
+            for p in range(nplane):
+                plane = ext1[p, piece, :]
+                gathered = jnp.where(lane // 2 == 2 * p, roll(plane, 4 * p + 3, 1), gathered)
+                gathered = jnp.where(lane // 2 == 2 * p + 1, roll(plane, 4 * p + 1, 1), gathered)
+            inner[piece, :] = gathered
+
+        for i, row in enumerate((PAD + 1, PAD + 2, top_row - 2, top_row - 3)):
+            for p in range(nplane):
+                edge_rows[i, pl.ds(p, 1), :] = ext1[p, pl.ds(row, 1), :]
+
+    @pl.when(lon == 0)
+    def _():
+        advance_block()
+
+    greetings = 3 + jnp.where(ne_self, 0, 1) + jnp.where(nw_self, 0, 1) + jnp.where(is_bottom, 0, 3)
+    pl.semaphore_wait(barrier, greetings)
+
+    @pl.when(ne_other)
+    def _():
+        go_ne.start()
+
+    @pl.when(nw_other)
+    def _():
+        go_nw.start()
+
+    @pl.when(not_bottom)
+    def _():
+        go_se.start()
+        go_sw.start()
+
+    go_w.start()
+    go_e.start()
+
+    for buf, first, second, corner in ((send_s, 0, 1, 0), (send_n, rows - 1, rows - 2, rows - 8)):
+        for at, row in ((0, first), (28, second)):
+            for p in range(nplane):
+                buf[pl.ds(at + p, 1), :] = ext0[p, pl.ds(PAD + row, 1), :]
+            for i in range(2):
+                buf[pl.ds(at + nplane + i, 1), :] = weights[i, pl.ds(row, 1), :]
+            buf[pl.ds(at + nplane + 2, 1), :] = scale[pl.ds(row, 1), :]
+            buf[pl.ds(at + nplane + 3, 1), :] = jnp.zeros((1, LANES), jnp.float32)
+        buf[pl.ds(56, 8), :] = packed[pl.ds(corner, 8), :]
+    go_n.start()
+
+    @pl.when(not_bottom)
+    def _():
+        go_s.start()
+
+    @pl.when(ne_self)
+    def _():
+        recv_c[3] = packed[pl.ds(rows - 8, 8), :]
+
+    @pl.when(nw_self)
+    def _():
+        recv_c[2] = packed[pl.ds(rows - 8, 8), :]
+
+    @pl.when(is_bottom)
+    def _():
+        recv_ns[0] = jnp.zeros(recv_ns.shape[1:], jnp.float32)
+        recv_c[0] = jnp.zeros(recv_c.shape[1:], jnp.float32)
+        recv_c[1] = jnp.zeros(recv_c.shape[1:], jnp.float32)
+
+    @pl.when(lon != 0)
+    def _():
+        advance_block()
 
     def arrived(dst, slot):
         remote(dst, dst, 0, slot, west, lat).wait_recv()

time: 14.2 us -> 13.8 us (0.972)
  Pallas kernels: 13.4 us -> 13 us
    pallas_call x1, Pallas kernels: 12.1 us -> 11.7 us  [local(): pl.pallas_call(first, out_shape=[pltpu.VMEM((nplane, rows, cols), f32), p...]
where the time goes in v7:
time: 13.8 us; the launch traced here: 13.7 us
  Pallas kernels  13 us (94%)
  between operations  0.66 us (5%)
    pallas_call x1, Pallas kernels, local(): pl.pallas_call(first, out_shape=[pltpu.VMEM((nplane, rows, cols), f32), p...  11.7 us
    pallas_call x1, Pallas kernels, local(): pl.pallas_call(second, out_shape=pltpu.HBM((nplane, rows, cols), f32), in...  1.32 us

profile of v7, /device:TPU:1, one launch (start us, length us, event | category | flops | bytes accessed | tf_op | source)
XLA Modules:
  0.0 13.7 jit_solution(11812399482637478610)
XLA Ops:
  0.7 11.7 %shard_map.55 = (f32[24,128,128]{2,1,0:T(8,128)S(1)}, f32[128,128]{1,0:T(8,128)S(1)}) custom-call(f32[24,128,128]{2,1,0:T(8,128)} %bitcast.2, f32[2,128,128]{2,1,0:T(8,128)} %refs_1_.1, f32[128,128]{1,0:T(8,128)} %refs_2_.1, s32[128,128]{1,0:T(8,128)} %refs_3_.1, s32[1,1]{1,0:T(1,128)S(6)} %copy.6.refs_4_), custom_call_target="tpu_custom_call" | custom-call | tf_op jit(solution)/shard_map/pallas_call | solution.py:517
  12.4 1.3 %shard_map.56 = f32[24,128,128]{2,1,0:T(8,128)} custom-call(f32[24,128,128]{2,1,0:T(8,128)S(1)} %get-tuple-element.7.refs_0_, f32[128,128]{1,0:T(8,128)S(1)} %get-tuple-element.8.refs_1_), custom_call_target="tpu_custom_call" | custom-call | tf_op jit(solution)/shard_map/pallas_call | solution.py:556

commit v8 on v7

--- a/solution.py
+++ b/solution.py
@@ -237,13 +237,36 @@
             for p in range(nplane):
                 edge_rows[i, pl.ds(p, 1), :] = ext1[p, pl.ds(row, 1), :]
 
+    def gather_rows():
+        for buf, first, second, corner in ((send_s, 0, 1, 0), (send_n, rows - 1, rows - 2, rows - 8)):
+            for at, row in ((0, first), (28, second)):
+                for p in range(nplane):
+                    buf[pl.ds(at + p, 1), :] = ext0[p, pl.ds(PAD + row, 1), :]
+                for i in range(2):
+                    buf[pl.ds(at + nplane + i, 1), :] = weights[i, pl.ds(row, 1), :]
+                buf[pl.ds(at + nplane + 2, 1), :] = scale[pl.ds(row, 1), :]
+                buf[pl.ds(at + nplane + 3, 1), :] = jnp.zeros((1, LANES), jnp.float32)
+            buf[pl.ds(56, 8), :] = packed[pl.ds(corner, 8), :]
+
+    def start_rows():
+        go_n.start()
+
+        @pl.when(not_bottom)
+        def _():
+            go_s.start()
+
     @pl.when(lon == 0)
     def _():
         advance_block()
+        gather_rows()
 
     greetings = 3 + jnp.where(ne_self, 0, 1) + jnp.where(nw_self, 0, 1) + jnp.where(is_bottom, 0, 3)
     pl.semaphore_wait(barrier, greetings)
 
+    @pl.when(lon == 0)
+    def _():
+        start_rows()
+
     @pl.when(ne_other)
     def _():
         go_ne.start()
@@ -260,20 +283,10 @@
     go_w.start()
     go_e.start()
 
-    for buf, first, second, corner in ((send_s, 0, 1, 0), (send_n, rows - 1, rows - 2, rows - 8)):
-        for at, row in ((0, first), (28, second)):
-            for p in range(nplane):
-                buf[pl.ds(at + p, 1), :] = ext0[p, pl.ds(PAD + row, 1), :]
-            for i in range(2):
-                buf[pl.ds(at + nplane + i, 1), :] = weights[i, pl.ds(row, 1), :]
-            buf[pl.ds(at + nplane + 2, 1), :] = scale[pl.ds(row, 1), :]
-            buf[pl.ds(at + nplane + 3, 1), :] = jnp.zeros((1, LANES), jnp.float32)
-        buf[pl.ds(56, 8), :] = packed[pl.ds(corner, 8), :]
-    go_n.start()
-
-    @pl.when(not_bottom)
-    def _():
-        go_s.start()
+    @pl.when(lon != 0)
+    def _():
+        gather_rows()
+        start_rows()
 
     @pl.when(ne_self)
     def _():

time: 13.8 us -> 13.7 us (level)
  no operation moved by 1% of the time
where the time goes in v8:
time: 13.7 us; the launch traced here: 13.6 us
  Pallas kernels  12.9 us (94%)
  between operations  0.66 us (5%)
    pallas_call x1, Pallas kernels, local(): pl.pallas_call(first, out_shape=[pltpu.VMEM((nplane, rows, cols), f32), p...  11.6 us
    pallas_call x1, Pallas kernels, local(): pl.pallas_call(second, out_shape=pltpu.HBM((nplane, rows, cols), f32), in...  1.32 us

profile of v8, /device:TPU:1, one launch (start us, length us, event | category | flops | bytes accessed | tf_op | source)
XLA Modules:
  0.0 13.6 jit_solution(15435913645524861602)
XLA Ops:
  0.7 11.6 %shard_map.55 = (f32[24,128,128]{2,1,0:T(8,128)S(1)}, f32[128,128]{1,0:T(8,128)S(1)}) custom-call(f32[24,128,128]{2,1,0:T(8,128)} %bitcast.2, f32[2,128,128]{2,1,0:T(8,128)} %refs_1_.1, f32[128,128]{1,0:T(8,128)} %refs_2_.1, s32[128,128]{1,0:T(8,128)} %refs_3_.1, s32[1,1]{1,0:T(1,128)S(6)} %copy.6.refs_4_), custom_call_target="tpu_custom_call" | custom-call | tf_op jit(solution)/shard_map/pallas_call | solution.py:530
  12.3 1.3 %shard_map.56 = f32[24,128,128]{2,1,0:T(8,128)} custom-call(f32[24,128,128]{2,1,0:T(8,128)S(1)} %get-tuple-element.7.refs_0_, f32[128,128]{1,0:T(8,128)S(1)} %get-tuple-element.8.refs_1_), custom_call_target="tpu_custom_call" | custom-call | tf_op jit(solution)/shard_map/pallas_call | solution.py:569
